TPU v7x, 32 devices: a whole 2x2x4 slice. The times are simulated.
32 devices in a mesh: groups: 2 (over x), ex: 16 (over z, y, core).
Axes of the slice: x: 2, y: 2, z: 4, core: 2. Of those that a mesh axis runs over, the one named last changes fastest.
Arguments:
- orbitals: bfloat16 [32768, 1024], P(('groups', 'ex')), parts along dimension 0, may hold values from -6 to 6
- element_blocks: bfloat16 [128, 256, 256], P(('groups', 'ex')), parts along dimension 0, may hold values from -0.25 to 6.75, as said below
- face_couplings: bfloat16 [3, 128, 256, 256], P(None, ('groups', 'ex')), parts along dimension 1, may hold values from -0.119628906 to 0.119628906
- face_order: int32 [3, 64, 256], P(None, 'ex'), may hold values from 0 to 255, each once within a row
Outputs:
- orthonormal: bfloat16 [32768, 1024], P(('groups', 'ex')), parts along dimension 0
There are 2 independent parts, one for each index of `groups`. A program takes and returns all parts, laid end to end along the dimension named above; an argument that names none is the same for every part. Nothing has to cross between parts.
Inputs may be any that keep to these rules, and one draw needn't show every extreme that they name: Each row of face_order names every one of 0 to 255 once. Each block of element_blocks is symmetric.
All inputs are finite; a program needn't handle non-finite values.
Results may differ from a plain program's by a relative error of at most 0.007.
Values may be sent and summed in bfloat16 or wider, within the bound.
A program may use at most 128 MiB of HBM per device.

v0:
```python
import jax
import jax.numpy as jnp
from jax import lax
from jax.sharding import PartitionSpec as P

EY = 2
EZ = 2


spectrum_top = 14.0
mean_epsilon = 1e-06


def from_behind(block, axis, distance):
    devices = range(lax.axis_size(axis))
    route = [((i - distance) % len(devices), i) for i in devices]
    return lax.ppermute(block, axis, route)


def extended(block, sides, width):
    for axis, dim in sides:
        count = lax.axis_size(axis)
        forward = [(i, i + 1) for i in range(count - 1)]
        forward.append((count - 1, 0))
        backward = [(target, source) for source, target in forward]
        low = lax.ppermute(
            lax.slice_in_dim(block, block.shape[dim] - width, None, axis=dim), axis, forward
        )
        high = lax.ppermute(lax.slice_in_dim(block, 0, width, axis=dim), axis, backward)
        block = jnp.concatenate([low, block, high], axis=dim)
    return block


def build_coupled(face_couplings, face_order):
    columns = jnp.arange(face_order.shape[-1], dtype=jnp.int32)
    selector = (face_order[:, :, :, None] == columns[None, None, None, :]).astype(jnp.bfloat16)
    return jnp.einsum(
        "deri,deic->derc", face_couplings, selector, preferred_element_type=jnp.float32
    ).astype(jnp.bfloat16)


def apply_blocks(blocks, coupled, next_faces, padded):
    centre = padded[1:-1]
    total = jnp.einsum("xyzij,xyzjc->xyzic", blocks, centre, preferred_element_type=jnp.float32)
    total = total + jnp.einsum(
        "xyzij,xyzjc->xyzic", coupled[0], padded[:-2], preferred_element_type=jnp.float32
    )
    total = total + jnp.einsum(
        "xyzji,xyzjc->xyzic", next_faces, padded[2:], preferred_element_type=jnp.float32
    )
    for axis_number in (1, 2):
        faces = coupled[axis_number]
        before = jnp.roll(centre, 1, axis_number)
        after = jnp.roll(centre, -1, axis_number)
        faces_after = jnp.roll(faces, -1, axis_number)
        total = total + jnp.einsum(
            "xyzij,xyzjc->xyzic", faces, before, preferred_element_type=jnp.float32
        )
        total = total + jnp.einsum(
            "xyzji,xyzjc->xyzic", faces_after, after, preferred_element_type=jnp.float32
        )
    return total


def filter_scalars(start_values, product, total_count):
    energy, weight = lax.psum(
        (jnp.sum(start_values * product), jnp.sum(start_values * start_values)), "ex"
    )
    cut_level = energy / total_count / (weight / total_count + mean_epsilon)
    return ((spectrum_top + cut_level) * 0.5, (spectrum_top - cut_level) * 0.5)


def on_device(orbitals, element_blocks, face_couplings, face_order):
    local_rows, orbital_count = orbitals.shape
    elements = element_blocks.shape[0]
    basis_size = element_blocks.shape[1]
    layers = elements // (EY * EZ)
    slab_rows = EY * EZ * basis_size
    total_rows = local_rows * lax.axis_size("ex")
    total_count = float(total_rows * orbital_count)
    coupled = build_coupled(face_couplings, face_order).reshape(
        3, layers, EY, EZ, basis_size, basis_size
    )
    blocks = element_blocks.reshape(layers, EY, EZ, basis_size, basis_size)
    beyond = from_behind(coupled[0, 0], "ex", -1)
    next_faces = jnp.concatenate([coupled[0, 1:], beyond[None]], axis=0)
    start_blocks = orbitals.reshape(layers, EY, EZ, basis_size, orbital_count)
    start_values = start_blocks.astype(jnp.float32)

    def neighbour_product(values):
        flat_values = values.reshape(local_rows, orbital_count)
        padded = extended(flat_values, (("ex", 0),), slab_rows)
        padded = padded.reshape(layers + 2, EY, EZ, basis_size, orbital_count)
        return apply_blocks(blocks, coupled, next_faces, padded)

    product = neighbour_product(start_blocks)
    center, half_width = filter_scalars(start_values, product, total_count)
    first_step = ((product - center * start_values) / half_width).astype(jnp.bfloat16)
    second_product = neighbour_product(first_step)
    filtered = (
        2.0 * (second_product - center * first_step.astype(jnp.float32)) / half_width - start_values
    ).astype(jnp.bfloat16)
    filtered = filtered.reshape(local_rows, orbital_count)
    summed_gram = lax.psum(
        jnp.einsum("rc,rd->cd", filtered, filtered, preferred_element_type=jnp.float32), "ex"
    )
    gram_matrix = summed_gram / float(total_rows)
    factor = jnp.linalg.cholesky(gram_matrix)
    solved = jax.scipy.linalg.solve_triangular(factor, filtered.astype(jnp.float32).T, lower=True)
    return solved.T.astype(jnp.bfloat16)


def solution(mesh):
    in_specs = (
        P(("groups", "ex"), None),
        P(("groups", "ex"), None, None),
        P(None, ("groups", "ex"), None, None),
        P(None, "ex", None),
    )
    out_specs = P(("groups", "ex"), None)
    return jax.shard_map(
        on_device, mesh=mesh, in_specs=in_specs, out_specs=out_specs, check_vma=False
    )
```

profile of v0, /device:TPU:0, one launch (start us, length us, event | category | flops | bytes accessed | tf_op | source)
XLA Modules:
  0.0 670.8 jit_solution(15889925304734490061)
XLA Ops:
  6.5 5.4 collective-permute-start.2
  13.5 4.5 collective-permute-start.1
  23.6 2.7 fusion.36
  26.3 14.2 %collective-permute-done = bf16[1024,1024]{1,0:T(8,128)(2,1)S(1)} collective-permute-done((bf16[1024,1024]{1,0:T(8,128)(2,1)}, bf16[1024,1024]{1,0:T(8,128)(2,1)S(1)}, u32[]{:S(2)}, u32[]{:S(2)}) %collective-permute-start) | collective-permute-done | bytes 2097184 | tf_op jit(solution)/shard_map/ppermute | solution.py:26
  40.5 2.7 fusion.112
  45.3 9.3 %fusion = (f32[]{:T(128)}, f32[2,2,256,1024]{3,2,1,0:T(8,128)}) fusion(bf16[2,2,256,1024]{3,2,1,0:T(8,128)(2,1)S(1)} %bitcast.195, f32[2,2,256,1024]{3,2,1,0:T(8,128)} %fusion.36, f32[2,2,256,1024]{3,2,1,0:T(8,128)S(1)} %fusion.37, f32[2,2,256,1024]{3,2,1,0:T(8,128)S(1)} %fusion.38, f32[2,2,256,1024]{3,2,1,0:T(8,128)S(1)} %fusion.39, ...), kind=kOutput, calls=%fused_computation.6 | convolution fusion | flops 546308096 | bytes 34078724 | tf_op jit(solution)/shard_map/xyzji,xyzjc->xyzic/dot_general | solution.py:48
  54.6 51.3 %all-reduce.1 = (f32[]{:T(128)}, f32[]{:T(128)}) all-reduce(f32[]{:T(128)} %get-tuple-element.79, f32[]{:T(128)} %multiply_reduce_fusion), channel_id=1, replica_groups=mesh['groups'=2,'ex'=16] {'ex'}, use_global_device_ids=true, to_apply=%region_1.2 | all-reduce | flops 2 | bytes 16 | tf_op jit(solution)/shard_map/psum | solution.py:66
  107.3 3.8 fusion.3
  115.7 2.7 fusion.35
  118.4 2.7 fusion.33
  121.2 2.7 fusion.114
  123.9 17.6 %collective-permute-done.3 = bf16[1024,1024]{1,0:T(8,128)(2,1)S(1)} collective-permute-done((bf16[1024,1024]{1,0:T(8,128)(2,1)S(1)}, bf16[1024,1024]{1,0:T(8,128)(2,1)S(1)}, u32[]{:S(2)}, u32[]{:S(2)}) %collective-permute-start.3) | collective-permute-done | bytes 2097184 | tf_op jit(solution)/shard_map/ppermute | solution.py:26
  141.5 2.7 fusion.113
  145.5 8.0 %fusion.4 = bf16[2,2,256,1024]{3,2,1,0:T(8,128)(2,1)S(1)} fusion(bf16[2,2,256,1024]{3,2,1,0:T(8,128)(2,1)S(1)} %fusion.3, f32[2,2,256,1024]{3,2,1,0:T(8,128)S(1)} %fusion.32, f32[2,2,256,1024]{3,2,1,0:T(8,128)} %fusion.33, f32[2,2,256,1024]{3,2,1,0:T(8,128)S(1)} %fusion.34, f32[2,2,256,1024]{3,2,1,0:T(8,128)} %fusion.35, f32[2,2,256,1024]{3,2,1,0:T(8,128)} %fusion.113, ...), kind=kOutput, calls=%fused_computation.10 | convolution fusion | flops 551550976 | bytes 34078728 | tf_op jit(solution)/shard_map/xyzji,xyzjc->xyzic/dot_general | solution.py:48
  154.8 4.4 convolution_bitcast_fusion
  159.3 4.0 bitcast_convert_fusion
  163.3 123.7 %all-reduce.4.cloned.1.call-done = f32[1024,1024]{0,1:T(8,128)} async-done(((f32[1024,1024]{0,1:T(8,128)}), f32[1024,1024]{0,1:T(8,128)}) %all-reduce.4.cloned.1.call-update) | async-done | bytes 4194320 | tf_op jit(solution)/shard_map/psum | solution.py:104
  287.0 5.0 broadcast_multiply_fusion
  291.9 5.6 copy.13
  297.5 4.4 fusion.5
  303.9 11.7 %cholesky.223 = f32[128,128]{1,0:T(8,128)S(1)} custom-call(f32[128,128]{1,0:T(8,128)S(1)} %cholesky.580), custom_call_target="Cholesky" | custom-call | tf_op jit(solution)/shard_map/jit(cholesky)/cholesky | solution.py:108
  315.7 9.8 %custom-call.63 = f32[1,128,128]{1,2,0:T(8,128)S(1)} custom-call(f32[1,128,128]{2,1,0:T(8,128)S(1)} %get-tuple-element.78), custom_call_target="InvertDiagBlocksLowerTriangular" | custom-call | tf_op jit(solution)/shard_map/jit(cholesky)/cholesky | solution.py:108
  325.5 2.5 cholesky.255
  328.0 2.3 constant_dynamic-update-slice_fusion.25
  331.9 12.1 %cholesky.244 = f32[128,128]{1,0:T(8,128)S(1)} custom-call(f32[128,128]{1,0:T(8,128)S(1)} %cholesky.584), custom_call_target="Cholesky" | custom-call | tf_op jit(solution)/shard_map/jit(cholesky)/cholesky | solution.py:108
  344.7 9.8 %custom-call.64 = f32[1,128,128]{1,2,0:T(8,128)S(1)} custom-call(f32[1,128,128]{2,1,0:T(8,128)S(1)} %get-tuple-element.75), custom_call_target="InvertDiagBlocksLowerTriangular" | custom-call | tf_op jit(solution)/shard_map/jit(cholesky)/cholesky | solution.py:108
  357.8 11.7 %cholesky.468 = f32[128,128]{1,0:T(8,128)S(1)} custom-call(f32[128,128]{1,0:T(8,128)S(1)} %cholesky.589), custom_call_target="Cholesky" | custom-call | tf_op jit(solution)/shard_map/jit(cholesky)/cholesky | solution.py:108
  370.9 9.8 %custom-call.65 = f32[1,128,128]{1,2,0:T(8,128)S(1)} custom-call(f32[1,128,128]{2,1,0:T(8,128)S(1)} %get-tuple-element.72), custom_call_target="InvertDiagBlocksLowerTriangular" | custom-call | tf_op jit(solution)/shard_map/jit(cholesky)/cholesky | solution.py:108
  384.2 11.9 %cholesky.487 = f32[128,128]{1,0:T(8,128)S(1)} custom-call(f32[128,128]{1,0:T(8,128)S(1)} %cholesky.594), custom_call_target="Cholesky" | custom-call | tf_op jit(solution)/shard_map/jit(cholesky)/cholesky | solution.py:108
  397.4 9.8 %custom-call.66 = f32[1,128,128]{1,2,0:T(8,128)S(1)} custom-call(f32[1,128,128]{2,1,0:T(8,128)S(1)} %get-tuple-element.69), custom_call_target="InvertDiagBlocksLowerTriangular" | custom-call | tf_op jit(solution)/shard_map/jit(cholesky)/cholesky | solution.py:108
  408.3 2.3 convolution_subtract_fusion.8
  410.7 11.7 %cholesky.506 = f32[128,128]{1,0:T(8,128)S(1)} custom-call(f32[128,128]{1,0:T(8,128)S(1)} %cholesky.599), custom_call_target="Cholesky" | custom-call | tf_op jit(solution)/shard_map/jit(cholesky)/cholesky | solution.py:108
  423.7 10.0 %custom-call.67 = f32[1,128,128]{1,2,0:T(8,128)S(1)} custom-call(f32[1,128,128]{2,1,0:T(8,128)S(1)} %get-tuple-element.66), custom_call_target="InvertDiagBlocksLowerTriangular" | custom-call | tf_op jit(solution)/shard_map/jit(cholesky)/cholesky | solution.py:108
  437.0 11.7 %cholesky.526 = f32[128,128]{1,0:T(8,128)S(1)} custom-call(f32[128,128]{1,0:T(8,128)S(1)} %cholesky.604), custom_call_target="Cholesky" | custom-call | tf_op jit(solution)/shard_map/jit(cholesky)/cholesky | solution.py:108
  450.0 9.8 %custom-call.68 = f32[1,128,128]{1,2,0:T(8,128)S(1)} custom-call(f32[1,128,128]{2,1,0:T(8,128)S(1)} %get-tuple-element.63), custom_call_target="InvertDiagBlocksLowerTriangular" | custom-call | tf_op jit(solution)/shard_map/jit(cholesky)/cholesky | solution.py:108
  462.8 12.1 %cholesky.546 = f32[128,128]{1,0:T(8,128)S(1)} custom-call(f32[128,128]{1,0:T(8,128)S(1)} %cholesky.609), custom_call_target="Cholesky" | custom-call | tf_op jit(solution)/shard_map/jit(cholesky)/cholesky | solution.py:108
  476.1 9.8 %custom-call.69 = f32[1,128,128]{1,2,0:T(8,128)S(1)} custom-call(f32[1,128,128]{2,1,0:T(8,128)S(1)} %get-tuple-element.60), custom_call_target="InvertDiagBlocksLowerTriangular" | custom-call | tf_op jit(solution)/shard_map/jit(cholesky)/cholesky | solution.py:108
  488.6 11.7 %cholesky.564 = f32[128,128]{1,0:T(8,128)S(1)} custom-call(f32[128,128]{1,0:T(8,128)S(1)} %convolution_subtract_fusion.11), custom_call_target="Cholesky" | custom-call | tf_op jit(solution)/shard_map/jit(cholesky)/cholesky | solution.py:108
  507.1 4.8 select_select_fusion
  512.0 23.7 %while.1 = (s32[]{:T(128)}, f32[1024,1024]{1,0:T(8,128)}, s32[8,2]{0,1:T(2,128)S(1)}, f32[8,128,128]{2,1,0:T(8,128)S(1)}, s32[]{:T(128)}) while((s32[]{:T(128)}, f32[1024,1024]{1,0:T(8,128)}, s32[8,2]{0,1:T(2,128)S(1)}, f32[8,128,128]{2,1,0:T(8,128)S(1)}, s32[]{:T(128)}) %tuple.62), condition=%wide.while_cond, body=%wide.while_body.sunk | while | flops 2 | bytes 131189 | solution.py:109
  535.7 78.8 %custom-call.70 = f32[8,128,128]{1,2,0:T(8,128)S(1)} custom-call(f32[8,128,128]{2,1,0:T(8,128)S(1)} %get-tuple-element.12), custom_call_target="InvertDiagBlocksLowerTriangular" | custom-call | tf_op jit(solution)/shard_map/jit(_solve_triangular)/triangular_solve | solution.py:109
  620.4 2.7 convolution_subtract_fusion
  624.5 3.6 fusion.40
  629.5 4.4 fusion.43
  636.1 5.6 convolution_subtract_fusion.2
  643.2 6.2 convolution_subtract_fusion.1
  650.8 7.5 %convolution_subtract_fusion.3 = f32[128,1024]{0,1:T(8,128)S(1)} fusion(f32[896,1024]{1,0:T(8,128)S(1)} %constant_dynamic-update-slice_fusion.11, f32[1024,1024]{0,1:T(8,128)S(1)} %copy-done.5, f32[1024,1024]{1,0:T(8,128)} %get-tuple-element.149), kind=kOutput, calls=%fused_computation.64 | convolution fusion | flops 1409417216 | bytes 5177344 | tf_op jit(solution)/shard_map/jit(_solve_triangular)/triangular_solve | solution.py:109
  659.6 3.9 copy.14
  (149 shorter events, 84.4 us)
Async XLA Ops:
  6.5 5.5 copy-start
  6.5 280.4 %all-reduce.4.cloned.1.call-start = ((), (), s32[]{:S(2)}) async-start(), calls=%async_computation | async-start | bytes 8388608 | tf_op jit(solution)/shard_map/psum | solution.py:104
  6.5 11.6 %copy-start.2 = (bf16[1024,1024]{1,0:T(8,128)(2,1)S(1)}, bf16[1024,1024]{1,0:T(8,128)(2,1)}, u32[]{:S(2)}) copy-start(bf16[1024,1024]{1,0:T(8,128)(2,1)} %param.4) | copy-start | bytes 6291460
  6.5 37.4 %collective-permute-start.2 = (bf16[1024,1024]{1,0:T(8,128)(2,1)}, bf16[1024,1024]{1,0:T(8,128)(2,1)S(1)}, u32[]{:S(2)}, u32[]{:S(2)}) collective-permute-start(bf16[1024,1024]{1,0:T(8,128)(2,1)} %param.4), channel_id=1, source_target_pairs={{1,0},{2,1},{3,2},{4,3},{5,4},{6,5},{7,6},{8,7},{9,8},{10,9},{11,1... | collective-permute-start | bytes 6291464 | tf_op jit(solution)/shard_map/ppermute | solution.py:29
  12.0 28.5 %collective-permute-start = (bf16[1024,1024]{1,0:T(8,128)(2,1)}, bf16[1024,1024]{1,0:T(8,128)(2,1)S(1)}, u32[]{:S(2)}, u32[]{:S(2)}) collective-permute-start(bf16[1024,1024]{1,0:T(8,128)(2,1)} %param.4), channel_id=1, source_target_pairs={{0,1},{1,2},{2,3},{3,4},{4,5},{5,6},{6,7},{7,8},{8,9},{9,10},{10,1... | collective-permute-start | bytes 6291464 | tf_op jit(solution)/shard_map/ppermute | solution.py:26
  13.5 26.9 %copy-start.8 = (bf16[1,4,256,256]{2,3,1,0:T(8,128)(2,1)}, bf16[1,4,256,256]{2,3,1,0:T(8,128)(2,1)S(1)}, u32[]{:S(2)}) copy-start(bf16[1,4,256,256]{2,3,1,0:T(8,128)(2,1)S(1)} %get-tuple-element.33) | copy-start | bytes 1572868
  13.5 29.6 %collective-permute-start.1 = (bf16[2,2,256,256]{2,3,1,0:T(8,128)(2,1)S(1)}, bf16[2,2,256,256]{2,3,1,0:T(8,128)(2,1)S(1)}, u32[]{:S(2)}, u32[]{:S(2)}) collective-permute-start(bf16[2,2,256,256]{2,3,1,0:T(8,128)(2,1)S(1)} %bitcast.205), channel_id=1, source_target_pairs={{1,0},{2,1},{3,2},{4,3},{5,4},{6,5},{7,6},{8,7},{9,8},{10,9},{11,1... | collective-permute-start | bytes 1572872 | tf_op jit(solution)/shard_map/ppermute | solution.py:17
  18.1 2.0 copy-start.10
  18.1 2.0 copy-start.12
  20.1 3.5 copy-start.14
  20.1 3.5 copy-start.16
  21.8 1.0 copy-start.22
  43.2 0.8 copy-start.18
  44.0 1.3 copy-start.20
  107.3 3.8 copy-start.3
  107.3 4.7 copy-start.4
  112.9 1.0 copy-start.11
  112.9 1.0 copy-start.13
  112.9 31.3 %collective-permute-start.4 = (bf16[1024,1024]{1,0:T(8,128)(2,1)S(1)}, bf16[1024,1024]{1,0:T(8,128)(2,1)S(1)}, u32[]{:S(2)}, u32[]{:S(2)}) collective-permute-start(bf16[1024,1024]{1,0:T(8,128)(2,1)S(1)} %bitcast.196), channel_id=1, source_target_pairs={{1,0},{2,1},{3,2},{4,3},{5,4},{6,5},{7,6},{8,7},{9,8},{10,9},{11,1... | collective-permute-start | bytes 6291464 | tf_op jit(solution)/shard_map/ppermute | solution.py:29
  113.0 28.5 %collective-permute-start.3 = (bf16[1024,1024]{1,0:T(8,128)(2,1)S(1)}, bf16[1024,1024]{1,0:T(8,128)(2,1)S(1)}, u32[]{:S(2)}, u32[]{:S(2)}) collective-permute-start(bf16[1024,1024]{1,0:T(8,128)(2,1)S(1)} %bitcast.197), channel_id=1, source_target_pairs={{0,1},{1,2},{2,3},{3,4},{4,5},{5,6},{6,7},{7,8},{8,9},{9,10},{10,1... | collective-permute-start | bytes 6291464 | tf_op jit(solution)/shard_map/ppermute | solution.py:26
  113.9 0.9 copy-start.15
  113.9 1.0 copy-start.17
  118.4 2.7 copy-start.23
  121.2 20.3 %copy-start.9 = (bf16[1,4,256,256]{2,3,1,0:T(8,128)(2,1)S(1)}, bf16[1,4,256,256]{2,3,1,0:T(8,128)(2,1)}, u32[]{:S(2)}) copy-start(bf16[1,4,256,256]{2,3,1,0:T(8,128)(2,1)} %copy-done.8) | copy-start | bytes 1572868
  123.9 21.7 %copy-start.19 = (bf16[2,2,256,256]{2,3,1,0:T(8,128)(2,1)S(1)}, bf16[2,2,256,256]{2,3,1,0:T(8,128)(2,1)}, u32[]{:S(2)}) copy-start(bf16[2,2,256,256]{2,3,1,0:T(8,128)(2,1)} %copy-done.18) | copy-start | bytes 1572868
  144.2 1.3 copy-start.21
  153.5 1.3 copy-start.7
  302.0 2.0 copy-start.6
  614.5 5.9 copy-start.5
  650.7 12.8 %copy-start.1 = (bf16[3,4,256,256]{3,2,1,0:T(8,128)(2,1)S(1)}, bf16[3,4,256,256]{3,2,1,0:T(8,128)(2,1)}, u32[]{:S(2)}) copy-start(bf16[3,4,256,256]{3,2,1,0:T(8,128)(2,1)} %param.6) | copy-start | bytes 4718596
Sparse Core Ops, SparseCore 0:
  159.4 127.5 all-reduce.3
where the time goes:
time: 680 us; the launch traced here: 671 us
  other arithmetic  276 us (41%)
  waiting for transfers between devices  155 us (23%)
  matrix products  111 us (16%)
  blocking collectives  51.3 us (8%)
  local copies, waits for them, and re-layouts  45.7 us (7%)
  between operations  20.7 us (3%)
  starting transfers between devices  10.6 us (2%)
    another operation x30, other arithmetic, on_device(): factor = jnp.linalg.cholesky(gram_matrix)  173 us
    psum x1, waiting for transfers between devices, on_device(): lax.psum(jnp.einsum('rc,rd->cd', filtered, filtered, preferred_element_ty...  124 us
    another operation x3, other arithmetic, on_device(): jax.scipy.linalg.solve_triangular(factor, filtered.astype(jnp.float32).T,...  83.6 us
    psum x1, blocking collectives, filter_scalars(): lax.psum((jnp.sum(start_values * product), jnp.sum(start_values * start_v...  51.3 us
    another operation x15, matrix products, on_device(): jax.scipy.linalg.solve_triangular(factor, filtered.astype(jnp.float32).T,...  43.9 us
    ppermute x2, waiting for transfers between devices, extended(): lax.ppermute(lax.slice_in_dim(block, block.shape[dim] - width, None, axis...  31.8 us
    another operation x24, local copies, waits for them, and re-layouts  23.6 us
    another operation x14, matrix products, on_device(): factor = jnp.linalg.cholesky(gram_matrix)  23.1 us
  transfers between devices with their start and end apart: 6, of which 3 were waited for; matrix products, arithmetic and copies ran while one was open for 4% of the time, Pallas kernels for 0%

commit v1 on v0

--- a/solution.py
+++ b/solution.py
@@ -1,10 +1,15 @@
+import functools
+
 import jax
 import jax.numpy as jnp
 from jax import lax
+from jax.experimental import pallas as pl
+from jax.experimental.pallas import tpu as pltpu
 from jax.sharding import PartitionSpec as P
 
 EY = 2
 EZ = 2
+BLOCK = 128
 
 
 spectrum_top = 14.0
@@ -68,6 +73,103 @@
     )
     cut_level = energy / total_count / (weight / total_count + mean_epsilon)
     return ((spectrum_top + cut_level) * 0.5, (spectrum_top - cut_level) * 0.5)
+
+
+def dot_split(a, b, dims):
+    a_high = a.astype(jnp.bfloat16)
+    a_low = (a - a_high.astype(jnp.float32)).astype(jnp.bfloat16)
+    b_high = b.astype(jnp.bfloat16)
+    b_low = (b - b_high.astype(jnp.float32)).astype(jnp.bfloat16)
+
+    def part(x, y):
+        return lax.dot_general(x, y, (dims, ((), ())), preferred_element_type=jnp.float32)
+
+    return part(a_high, b_high) + (part(a_high, b_low) + part(a_low, b_high))
+
+
+def inverse_factor(block):
+    tiles = BLOCK // 8
+    lane = lax.broadcasted_iota(jnp.int32, (1, BLOCK), 1)
+    sub = lax.broadcasted_iota(jnp.int32, (8, 1), 0)
+
+    def group(step, state):
+        state = list(state)
+        for j in range(8):
+            here = lane == j
+            head = state[0]
+            pivot = head[j : j + 1, j : j + 1]
+            scale = lax.rsqrt(pivot)
+            row = jnp.where(here, 1.0, head[j : j + 1, :])
+            scaled = row * scale
+            used = scaled * scale
+            for t in range(tiles):
+                column = state[t][:, j : j + 1]
+                if t == 0:
+                    column = jnp.where(sub > j, column, 0.0)
+                    kept = jnp.where(here & (sub > j), 0.0, state[t])
+                    new = kept - column * used
+                    state[t] = jnp.where(sub == j, scaled, new)
+                else:
+                    live = t < tiles - step
+                    new = jnp.where(here, 0.0, state[t]) - column * used
+                    state[t] = jnp.where(live, new, state[t])
+        state = [pltpu.roll(x, BLOCK - 8, 1) for x in state]
+        return tuple(state[1:] + state[:1])
+
+    state = tuple(block[8 * t : 8 * t + 8, :] for t in range(tiles))
+    state = lax.fori_loop(0, tiles, group, state)
+    full = jnp.concatenate(state, axis=0)
+    rows = lax.broadcasted_iota(jnp.int32, (BLOCK, BLOCK), 0)
+    columns = lax.broadcasted_iota(jnp.int32, (BLOCK, BLOCK), 1)
+    return jnp.where(columns <= rows, full, 0.0)
+
+
+def orthonormal_kernel(row_count, gram_ref, filtered_ref, out_ref, work):
+    size = gram_ref.shape[0]
+    work[...] = gram_ref[...] * (1.0 / row_count)
+    for start in range(0, size, BLOCK):
+        stop = start + BLOCK
+        inverse = inverse_factor(work[start:stop, start:stop])
+        if start > 0:
+            work[start:stop, :start] = dot_split(inverse, work[start:stop, :start], ((1,), (0,)))
+        work[start:stop, start:stop] = inverse
+        if stop < size:
+            upper = dot_split(inverse, work[start:stop, stop:], ((1,), (0,)))
+            work[start:stop, stop:] = upper
+            work[stop:, start:stop] = jnp.zeros((size - stop, BLOCK), jnp.float32)
+            lower = upper.T
+            for column in range(0, size, 256):
+                work[stop:, column : column + 256] -= dot_split(
+                    lower, work[start:stop, column : column + 256], ((1,), (0,))
+                )
+    for start in range(0, size, 256):
+        stop = start + 256
+        rows = lax.broadcasted_iota(jnp.int32, (256, stop), 0) + start
+        columns = lax.broadcasted_iota(jnp.int32, (256, stop), 1)
+        wide = jnp.where(columns <= rows, work[start:stop, :stop], 0.0)
+        high = wide.astype(jnp.bfloat16)
+        low = (wide - high.astype(jnp.float32)).astype(jnp.bfloat16)
+        total = lax.dot_general(
+            filtered_ref[:, :stop], high, (((1,), (1,)), ((), ())),
+            preferred_element_type=jnp.float32,
+        )
+        total = total + lax.dot_general(
+            filtered_ref[:, :stop], low, (((1,), (1,)), ((), ())),
+            preferred_element_type=jnp.float32,
+        )
+        out_ref[:, start:stop] = total.astype(jnp.bfloat16)
+
+
+def orthonormalize(summed_gram, filtered, row_count):
+    whole = pl.BlockSpec(memory_space=pltpu.VMEM)
+    return pl.pallas_call(
+        functools.partial(orthonormal_kernel, float(row_count)),
+        out_shape=jax.ShapeDtypeStruct(filtered.shape, jnp.bfloat16),
+        in_specs=[whole, whole],
+        out_specs=whole,
+        scratch_shapes=[pltpu.VMEM(summed_gram.shape, jnp.float32)],
+        compiler_params=pltpu.CompilerParams(vmem_limit_bytes=48 * 1024 * 1024),
+    )(summed_gram, filtered)
 
 
 def on_device(orbitals, element_blocks, face_couplings, face_order):
@@ -104,10 +206,7 @@
     summed_gram = lax.psum(
         jnp.einsum("rc,rd->cd", filtered, filtered, preferred_element_type=jnp.float32), "ex"
     )
-    gram_matrix = summed_gram / float(total_rows)
-    factor = jnp.linalg.cholesky(gram_matrix)
-    solved = jax.scipy.linalg.solve_triangular(factor, filtered.astype(jnp.float32).T, lower=True)
-    return solved.T.astype(jnp.bfloat16)
+    return orthonormalize(summed_gram, filtered, total_rows)
 
 
 def solution(mesh):

time: 680 us -> 409 us (0.60); the launches traced: 671 us -> 409 us
  other arithmetic: 276 us -> 6.5 us
  Pallas kernels: 0 us -> 113 us
  matrix products: 111 us -> 44.1 us
  local copies, waits for them, and re-layouts: 45.7 us -> 9.52 us
    another operation x33 -> x0, other arithmetic: 256 us -> none  [the longest x30 173 us: on_device(): factor = jnp.linalg.cholesky(gram_matrix)]
    pallas_call x0 -> x1, Pallas kernels: none -> 113 us  [orthonormalize(): pl.pallas_call(functools.partial(orthonormal_kernel, float(row_count)), o...]
    another operation x29 -> x0, matrix products: 67 us -> none  [the longest x15 43.9 us: on_device(): jax.scipy.linalg.solve_triangular(factor, filtered.astype(jnp.float32).T,...]
    another operation x34 -> x0, local copies, waits for them, and re-layouts: 26.2 us -> none
    div x2 -> x0, other arithmetic: 9.42 us -> none  [the longest x1 4.97 us: on_device(): gram_matrix = summed_gram / float(total_rows)]
  transfers between devices with their start and end apart: 6 -> 6, of which waited for: 3 -> 3; matrix products, arithmetic and copies ran while one was open for 4% -> 6% of each run, Pallas kernels for 0% -> 0%
where the time goes in v1:
time: 409 us
  waiting for transfers between devices  159 us (39%)
  Pallas kernels  113 us (28%)
  blocking collectives  51.3 us (13%)
  matrix products  44.1 us (11%)
  between operations  15.1 us (4%)
  starting transfers between devices  10.6 us (3%)
  local copies, waits for them, and re-layouts  9.52 us (2%)
  other arithmetic  6.5 us (2%)
    psum x1, waiting for transfers between devices, on_device(): lax.psum(jnp.einsum('rc,rd->cd', filtered, filtered, preferred_element_ty...  128 us
    pallas_call x1, Pallas kernels, orthonormalize(): pl.pallas_call(functools.partial(orthonormal_kernel, float(row_count)), o...  113 us
    psum x1, blocking collectives, filter_scalars(): lax.psum((jnp.sum(start_values * product), jnp.sum(start_values * start_v...  51.3 us
    ppermute x2, waiting for transfers between devices, extended(): lax.ppermute(lax.slice_in_dim(block, block.shape[dim] - width, None, axis...  30.9 us
    dot_general x2, matrix products, apply_blocks(): jnp.einsum('xyzji,xyzjc->xyzic', next_faces, padded[2:], preferred_elemen...  17.3 us
    unnamed x46, local copies, waits for them, and re-layouts  8.66 us
  transfers between devices with their start and end apart: 6, of which 3 were waited for; matrix products, arithmetic and copies ran while one was open for 6% of the time, Pallas kernels for 0%

profile of v1, /device:TPU:0, one launch (start us, length us, event | category | flops | bytes accessed | tf_op | source)
XLA Modules:
  0.0 408.8 jit_solution(17424237945507972888)
XLA Ops:
  6.5 5.4 %collective-permute-start.2 = (bf16[1024,1024]{1,0:T(8,128)(2,1)}, bf16[1024,1024]{1,0:T(8,128)(2,1)S(1)}, u32[]{:S(2)}, u32[]{:S(2)}) collective-permute-start(bf16[1024,1024]{1,0:T(8,128)(2,1)} %param.4), channel_id=1, source_target_pairs={{1,0},{2,1},{3,2},{4,3},{5,4},{6,5},{7,6},{8,7},{9,8},{10,9},{11,1... | collective-permute-start | bytes 6291464 | tf_op jit(solution)/shard_map/ppermute | solution.py:34
  12.0 0.0 collective-permute-start
  12.0 1.4 fusion.16
  13.4 0.1 fusion.37
  13.5 4.5 %collective-permute-start.1 = (bf16[2,2,256,256]{2,3,1,0:T(8,128)(2,1)S(1)}, bf16[2,2,256,256]{2,3,1,0:T(8,128)(2,1)S(1)}, u32[]{:S(2)}, u32[]{:S(2)}) collective-permute-start(bf16[2,2,256,256]{2,3,1,0:T(8,128)(2,1)S(1)} %bitcast.102), channel_id=1, source_target_pairs={{1,0},{2,1},{3,2},{4,3},{5,4},{6,5},{7,6},{8,7},{9,8},{10,9},{11,1... | collective-permute-start | bytes 1572872 | tf_op jit(solution)/shard_map/ppermute | solution.py:22
  18.1 0.2 fusion.35
  18.3 1.8 multiply_reduce_fusion
  20.1 0.7 fusion.23
  20.9 0.2 fusion.36
  21.0 0.8 fusion.24
  21.8 0.0 copy-start.21
  21.8 0.8 fusion.22
  22.6 0.3 copy-done.21
  22.8 0.7 fusion.40
  23.6 2.8 fusion.21
  26.4 14.1 %collective-permute-done = bf16[1024,1024]{1,0:T(8,128)(2,1)S(1)} collective-permute-done((bf16[1024,1024]{1,0:T(8,128)(2,1)}, bf16[1024,1024]{1,0:T(8,128)(2,1)S(1)}, u32[]{:S(2)}, u32[]{:S(2)}) %collective-permute-start) | collective-permute-done | bytes 2097184 | tf_op jit(solution)/shard_map/ppermute | solution.py:31
  40.5 2.7 fusion.41
  43.2 0.8 copy-done.17
  44.0 1.3 copy-done.19
  45.3 9.4 %fusion = (f32[]{:T(128)}, f32[2,2,256,1024]{3,2,1,0:T(8,128)}) fusion(bf16[2,2,256,1024]{3,2,1,0:T(8,128)(2,1)S(1)} %bitcast.93, f32[2,2,256,1024]{3,2,1,0:T(8,128)} %fusion.21, f32[2,2,256,1024]{3,2,1,0:T(8,128)S(1)} %fusion.22, f32[2,2,256,1024]{3,2,1,0:T(8,128)S(1)} %fusion.23, f32[2,2,256,1024]{3,2,1,0:T(8,128)S(1)} %fusion.24, ...), kind=kOutput, calls=%fused_computation.3 | convolution fusion | flops 546308096 | bytes 34078724 | tf_op jit(solution)/shard_map/xyzji,xyzjc->xyzic/dot_general | solution.py:53
  54.7 51.3 %all-reduce = (f32[]{:T(128)}, f32[]{:T(128)}) all-reduce(f32[]{:T(128)} %get-tuple-element.22, f32[]{:T(128)} %multiply_reduce_fusion), channel_id=1, replica_groups=mesh['groups'=2,'ex'=16] {'ex'}, use_global_device_ids=true, to_apply=%region_1.2 | all-reduce | flops 2 | bytes 16 | tf_op jit(solution)/shard_map/psum | solution.py:71
  107.3 0.0 copy-start.5
  107.4 3.8 fusion.3
  111.2 0.8 copy-done.6
  112.0 0.9 fusion.63
  113.0 0.1 collective-permute-start.4
  113.1 0.6 collective-permute-start.3
  113.6 0.2 fusion.33
  113.8 0.1 copy-done.10
  113.9 0.1 copy-done.12
  114.0 0.7 fusion.19
  114.8 0.2 fusion.34
  114.9 0.8 copy-done.14
  115.7 0.1 copy-done.16
  115.8 0.7 fusion.17
  116.5 2.8 fusion.20
  119.3 2.7 fusion.18
  122.0 2.7 fusion.43
  124.7 16.8 %collective-permute-done.3 = bf16[1024,1024]{1,0:T(8,128)(2,1)S(1)} collective-permute-done((bf16[1024,1024]{1,0:T(8,128)(2,1)S(1)}, bf16[1024,1024]{1,0:T(8,128)(2,1)S(1)}, u32[]{:S(2)}, u32[]{:S(2)}) %collective-permute-start.3) | collective-permute-done | bytes 2097184 | tf_op jit(solution)/shard_map/ppermute | solution.py:31
  141.6 2.7 fusion.42
  144.3 1.3 copy-done.20
  145.6 8.0 %fusion.4 = bf16[2,2,256,1024]{3,2,1,0:T(8,128)(2,1)S(1)} fusion(bf16[2,2,256,1024]{3,2,1,0:T(8,128)(2,1)S(1)} %fusion.3, f32[2,2,256,1024]{3,2,1,0:T(8,128)S(1)} %fusion.17, f32[2,2,256,1024]{3,2,1,0:T(8,128)} %fusion.18, f32[2,2,256,1024]{3,2,1,0:T(8,128)S(1)} %fusion.19, f32[2,2,256,1024]{3,2,1,0:T(8,128)} %fusion.20, f32[2,2,256,1024]{3,2,1,0:T(8,128)} %fusion.42, ...), kind=kOutput, calls=%fused_computation.7 | convolution fusion | flops 551550976 | bytes 34078728 | tf_op jit(solution)/shard_map/xyzji,xyzjc->xyzic/dot_general | solution.py:53
  153.6 4.5 %convolution_bitcast_fusion = f32[1024,1024]{1,0:T(8,128)} fusion(bf16[2,2,256,1024]{3,2,1,0:T(8,128)(2,1)S(1)} %fusion.4), kind=kOutput, calls=%fused_computation.21 | convolution fusion | flops 2147483648 | bytes 6291456 | tf_op jit(solution)/shard_map/rc,rd->cd/dot_general | solution.py:207
  158.1 1.3 copy-done.2
  159.4 0.0 all-reduce.3.cloned.1.call-update
  159.4 127.8 %all-reduce.3.cloned.1.call-done.gram_ref = f32[1024,1024]{1,0:T(8,128)} async-done(((f32[1024,1024]{1,0:T(8,128)}), f32[1024,1024]{1,0:T(8,128)}) %all-reduce.3.cloned.1.call-update) | async-done | bytes 4194320 | tf_op jit(solution)/shard_map/psum | solution.py:206
  287.2 1.7 copy-done.3
  288.9 113.0 %shard_map.46 = bf16[1024,1024]{1,0:T(8,128)(2,1)} custom-call(f32[1024,1024]{1,0:T(8,128)} %all-reduce.3.cloned.1.call-done.gram_ref, bf16[1024,1024]{1,0:T(8,128)(2,1)S(1)} %bitcast.89), custom_call_target="tpu_custom_call" | custom-call | tf_op jit(solution)/shard_map/pallas_call | solution.py:165
  (39 shorter events, 0.1 us)
Async XLA Ops:
  6.5 5.5 %copy-start = (bf16[3,4,256,256]{3,2,1,0:T(8,128)(2,1)S(1)}, bf16[3,4,256,256]{3,2,1,0:T(8,128)(2,1)}, u32[]{:S(2)}) copy-start(bf16[3,4,256,256]{3,2,1,0:T(8,128)(2,1)} %param.6) | copy-start | bytes 4718596
  6.5 280.7 %all-reduce.3.cloned.1.call-start = ((), (), s32[]{:S(2)}) async-start(), calls=%async_computation | async-start | bytes 8388608 | tf_op jit(solution)/shard_map/psum | solution.py:206
  6.5 11.6 %copy-start.4 = (bf16[1024,1024]{1,0:T(8,128)(2,1)S(1)}, bf16[1024,1024]{1,0:T(8,128)(2,1)}, u32[]{:S(2)}) copy-start(bf16[1024,1024]{1,0:T(8,128)(2,1)} %param.4) | copy-start | bytes 6291460
  6.5 37.5 %collective-permute-start.2 = (bf16[1024,1024]{1,0:T(8,128)(2,1)}, bf16[1024,1024]{1,0:T(8,128)(2,1)S(1)}, u32[]{:S(2)}, u32[]{:S(2)}) collective-permute-start(bf16[1024,1024]{1,0:T(8,128)(2,1)} %param.4), channel_id=1, source_target_pairs={{1,0},{2,1},{3,2},{4,3},{5,4},{6,5},{7,6},{8,7},{9,8},{10,9},{11,1... | collective-permute-start | bytes 6291464 | tf_op jit(solution)/shard_map/ppermute | solution.py:34
  12.0 28.5 %collective-permute-start = (bf16[1024,1024]{1,0:T(8,128)(2,1)}, bf16[1024,1024]{1,0:T(8,128)(2,1)S(1)}, u32[]{:S(2)}, u32[]{:S(2)}) collective-permute-start(bf16[1024,1024]{1,0:T(8,128)(2,1)} %param.4), channel_id=1, source_target_pairs={{0,1},{1,2},{2,3},{3,4},{4,5},{5,6},{6,7},{7,8},{8,9},{9,10},{10,1... | collective-permute-start | bytes 6291464 | tf_op jit(solution)/shard_map/ppermute | solution.py:31
  13.5 26.9 %copy-start.7 = (bf16[1,4,256,256]{2,3,1,0:T(8,128)(2,1)}, bf16[1,4,256,256]{2,3,1,0:T(8,128)(2,1)S(1)}, u32[]{:S(2)}) copy-start(bf16[1,4,256,256]{2,3,1,0:T(8,128)(2,1)S(1)} %get-tuple-element.15) | copy-start | bytes 1572868
  13.5 29.6 %collective-permute-start.1 = (bf16[2,2,256,256]{2,3,1,0:T(8,128)(2,1)S(1)}, bf16[2,2,256,256]{2,3,1,0:T(8,128)(2,1)S(1)}, u32[]{:S(2)}, u32[]{:S(2)}) collective-permute-start(bf16[2,2,256,256]{2,3,1,0:T(8,128)(2,1)S(1)} %bitcast.102), channel_id=1, source_target_pairs={{1,0},{2,1},{3,2},{4,3},{5,4},{6,5},{7,6},{8,7},{9,8},{10,9},{11,1... | collective-permute-start | bytes 1572872 | tf_op jit(solution)/shard_map/ppermute | solution.py:22
  18.1 2.0 copy-start.9
  18.1 2.0 copy-start.11
  20.1 3.5 copy-start.13
  20.1 3.5 copy-start.15
  21.8 1.0 copy-start.21
  43.2 0.8 copy-start.17
  44.0 1.3 copy-start.19
  107.3 3.8 copy-start.5
  107.4 4.7 %copy-start.6 = (f32[2,2,256,1024]{3,2,1,0:T(8,128)S(1)}, f32[2,2,256,1024]{3,2,1,0:T(8,128)}, u32[]{:S(2)}) copy-start(f32[2,2,256,1024]{3,2,1,0:T(8,128)} %get-tuple-element.23) | copy-start | bytes 12582916
  113.0 1.0 copy-start.10
  113.0 1.0 copy-start.12
  113.0 31.3 %collective-permute-start.4 = (bf16[1024,1024]{1,0:T(8,128)(2,1)S(1)}, bf16[1024,1024]{1,0:T(8,128)(2,1)S(1)}, u32[]{:S(2)}, u32[]{:S(2)}) collective-permute-start(bf16[1024,1024]{1,0:T(8,128)(2,1)S(1)} %bitcast.94), channel_id=1, source_target_pairs={{1,0},{2,1},{3,2},{4,3},{5,4},{6,5},{7,6},{8,7},{9,8},{10,9},{11,1... | collective-permute-start | bytes 6291464 | tf_op jit(solution)/shard_map/ppermute | solution.py:34
  113.1 28.5 %collective-permute-start.3 = (bf16[1024,1024]{1,0:T(8,128)(2,1)S(1)}, bf16[1024,1024]{1,0:T(8,128)(2,1)S(1)}, u32[]{:S(2)}, u32[]{:S(2)}) collective-permute-start(bf16[1024,1024]{1,0:T(8,128)(2,1)S(1)} %bitcast.95), channel_id=1, source_target_pairs={{0,1},{1,2},{2,3},{3,4},{4,5},{5,6},{6,7},{7,8},{8,9},{9,10},{10,1... | collective-permute-start | bytes 6291464 | tf_op jit(solution)/shard_map/ppermute | solution.py:31
  114.7 1.0 copy-start.14
  114.8 1.0 copy-start.16
  119.3 2.7 copy-start.22
  122.0 19.5 %copy-start.8 = (bf16[1,4,256,256]{2,3,1,0:T(8,128)(2,1)S(1)}, bf16[1,4,256,256]{2,3,1,0:T(8,128)(2,1)}, u32[]{:S(2)}) copy-start(bf16[1,4,256,256]{2,3,1,0:T(8,128)(2,1)} %copy-done.7) | copy-start | bytes 1572868
  141.6 4.0 copy-start.18
  144.3 1.3 copy-start.20
  158.1 1.3 copy-start.2
  287.2 114.7 %copy-start.1 = (bf16[3,4,256,256]{3,2,1,0:T(8,128)(2,1)S(1)}, bf16[3,4,256,256]{3,2,1,0:T(8,128)(2,1)}, u32[]{:S(2)}) copy-start(bf16[3,4,256,256]{3,2,1,0:T(8,128)(2,1)} %param.6) | copy-start | bytes 4718596
  287.2 1.7 copy-start.3
Sparse Core Ops, SparseCore 0:
  159.5 127.6 all-reduce.2

commit v2 on v1

--- a/solution.py
+++ b/solution.py
@@ -68,8 +68,8 @@
 
 
 def filter_scalars(start_values, product, total_count):
-    energy, weight = lax.psum(
-        (jnp.sum(start_values * product), jnp.sum(start_values * start_values)), "ex"
+    energy, weight = sum_scalars(
+        jnp.sum(start_values * product), jnp.sum(start_values * start_values)
     )
     cut_level = energy / total_count / (weight / total_count + mean_epsilon)
     return ((spectrum_top + cut_level) * 0.5, (spectrum_top - cut_level) * 0.5)
@@ -124,9 +124,169 @@
     return jnp.where(columns <= rows, full, 0.0)
 
 
+def partner_of(me, bit):
+    distance = 1 << bit
+    side = lax.rem(lax.div(me, distance), 2)
+    return me + distance * (1 - 2 * side), side
+
+
+def greet(axis, bits):
+    me = lax.axis_index(axis)
+    barrier = pltpu.get_barrier_semaphore()
+    for bit in bits:
+        other, _ = partner_of(me, bit)
+        pl.semaphore_signal(
+            barrier, inc=1, device_id={axis: other}, device_id_type=pl.DeviceIdType.MESH
+        )
+    pl.semaphore_wait(barrier, len(bits))
+    return me
+
+
+def scalar_sum_kernel(bits, own_ref, out_ref, held, landed, send_sem, recv_sem):
+    me = greet("ex", bits)
+    held[0] = own_ref[...]
+    for step, bit in enumerate(bits):
+        other, _ = partner_of(me, bit)
+        copy = pltpu.make_async_remote_copy(
+            src_ref=held.at[step],
+            dst_ref=landed.at[step],
+            send_sem=send_sem.at[step],
+            recv_sem=recv_sem.at[step],
+            device_id={"ex": other},
+            device_id_type=pl.DeviceIdType.MESH,
+        )
+        copy.start()
+        copy.wait()
+        held[step + 1] = held[step] + landed[step]
+    out_ref[...] = held[len(bits)]
+
+
+def bits_of(axis):
+    count = lax.axis_size(axis)
+    return list(range(count.bit_length() - 1))
+
+
+def sum_scalars(first, second):
+    bits = bits_of("ex")
+    rows = lax.broadcasted_iota(jnp.int32, (8, 128), 0)
+    own = jnp.where(rows < 4, first, second)
+    whole = pl.BlockSpec(memory_space=pltpu.VMEM)
+    total = pl.pallas_call(
+        functools.partial(scalar_sum_kernel, bits),
+        out_shape=jax.ShapeDtypeStruct((8, 128), jnp.float32),
+        in_specs=[whole],
+        out_specs=whole,
+        scratch_shapes=[
+            pltpu.VMEM((len(bits) + 1, 8, 128), jnp.float32),
+            pltpu.VMEM((len(bits), 8, 128), jnp.float32),
+            pltpu.SemaphoreType.DMA((len(bits),)),
+            pltpu.SemaphoreType.DMA((len(bits),)),
+        ],
+        compiler_params=pltpu.CompilerParams(collective_id=0, has_side_effects=True),
+    )(own)
+    return total[0, 0], total[4, 0]
+
+
+def gram_sum_kernel(streams, gram_ref, out_ref, work, landed, send_sem, recv_sem):
+    me = greet("ex", sorted(streams[0][2]))
+    blocks = gram_ref.shape[0] // BLOCK
+    place = 0
+    for i in range(blocks):
+        for j in range(i + 1):
+            tile = gram_ref[i * BLOCK : (i + 1) * BLOCK, j * BLOCK : (j + 1) * BLOCK]
+            work[place : place + BLOCK // 8] = tile.reshape(BLOCK // 8, 8, 128)
+            place += BLOCK // 8
+    steps = len(streams[0][2])
+    offsets = [start for start, _, _ in streams]
+    lengths = [length for _, length, _ in streams]
+    landings = [start for start, _, _ in streams]
+
+    def send(s, source, target, number, other):
+        copy = pltpu.make_async_remote_copy(
+            src_ref=source,
+            dst_ref=target,
+            send_sem=send_sem.at[s, number],
+            recv_sem=recv_sem.at[s, number],
+            device_id={"ex": other},
+            device_id_type=pl.DeviceIdType.MESH,
+        )
+        copy.start()
+        return copy
+
+    def scatter(s, step):
+        other, side = partner_of(me, streams[s][2][step])
+        half = lengths[s] // 2
+        given = offsets[s] + (1 - side) * half
+        lengths[s] = half
+        offsets[s] = offsets[s] + side * half
+        landing = landings[s]
+        landings[s] = landing + half
+        copy = send(s, work.at[pl.ds(given, half)], landed.at[pl.ds(landing, half)], step, other)
+        return copy, landing
+
+    def gather(s, step):
+        bit = streams[s][2][steps - 1 - step]
+        other, side = partner_of(me, bit)
+        here = pl.ds(offsets[s], lengths[s])
+        copy = send(s, out_ref.at[here], out_ref.at[here], steps + step, other)
+        offsets[s] = offsets[s] - side * lengths[s]
+        lengths[s] = lengths[s] * 2
+        return copy
+
+    several = range(len(streams))
+    flying = [scatter(s, 0) for s in several]
+    for step in range(steps):
+        for s in several:
+            copy, landing = flying[s]
+            copy.wait()
+            kept = pl.ds(offsets[s], lengths[s])
+            total = work[kept] + landed[landing : landing + lengths[s]]
+            if step + 1 < steps:
+                work[kept] = total
+                flying[s] = scatter(s, step + 1)
+            else:
+                out_ref[kept] = total
+                flying[s] = gather(s, 0)
+    for step in range(steps):
+        for s in several:
+            flying[s].wait()
+            if step + 1 < steps:
+                flying[s] = gather(s, step + 1)
+
+
+def sum_gram(gram):
+    bits = bits_of("ex")
+    count = lax.axis_size("ex")
+    blocks = gram.shape[0] // BLOCK
+    tiles = blocks * (blocks + 1) // 2 * (BLOCK // 8)
+    cut = tiles // count // 2 * count
+    streams = [(0, cut, bits), (cut, tiles - cut, bits[:1] + bits[2:] + bits[1:2])]
+    whole = pl.BlockSpec(memory_space=pltpu.VMEM)
+    return pl.pallas_call(
+        functools.partial(gram_sum_kernel, streams),
+        out_shape=jax.ShapeDtypeStruct((tiles, 8, 128), jnp.float32),
+        in_specs=[whole],
+        out_specs=whole,
+        scratch_shapes=[
+            pltpu.VMEM((tiles, 8, 128), jnp.float32),
+            pltpu.VMEM((tiles, 8, 128), jnp.float32),
+            pltpu.SemaphoreType.DMA((2, 2 * len(bits))),
+            pltpu.SemaphoreType.DMA((2, 2 * len(bits))),
+        ],
+        compiler_params=pltpu.CompilerParams(
+            collective_id=1, has_side_effects=True, vmem_limit_bytes=32 * 1024 * 1024
+        ),
+    )(gram)
+
+
 def orthonormal_kernel(row_count, gram_ref, filtered_ref, out_ref, work):
-    size = gram_ref.shape[0]
-    work[...] = gram_ref[...] * (1.0 / row_count)
+    size = work.shape[0]
+    place = 0
+    for i in range(size // BLOCK):
+        for j in range(i + 1):
+            tile = gram_ref[place : place + BLOCK // 8].reshape(BLOCK, BLOCK)
+            work[i * BLOCK : (i + 1) * BLOCK, j * BLOCK : (j + 1) * BLOCK] = tile * (1.0 / row_count)
+            place += BLOCK // 8
     for start in range(0, size, BLOCK):
         stop = start + BLOCK
         inverse = inverse_factor(work[start:stop, start:stop])
@@ -134,13 +294,13 @@
             work[start:stop, :start] = dot_split(inverse, work[start:stop, :start], ((1,), (0,)))
         work[start:stop, start:stop] = inverse
         if stop < size:
-            upper = dot_split(inverse, work[start:stop, stop:], ((1,), (0,)))
-            work[start:stop, stop:] = upper
+            lower = dot_split(work[stop:, start:stop], inverse, ((1,), (1,)))
+            work[start:stop, stop:] = lower.T
             work[stop:, start:stop] = jnp.zeros((size - stop, BLOCK), jnp.float32)
-            lower = upper.T
-            for column in range(0, size, 256):
-                work[stop:, column : column + 256] -= dot_split(
-                    lower, work[start:stop, column : column + 256], ((1,), (0,))
+            for column in range(0, size, BLOCK):
+                first = max(stop, column)
+                work[first:, column : column + BLOCK] -= dot_split(
+                    lower[first - stop :], work[start:stop, column : column + BLOCK], ((1,), (0,))
                 )
     for start in range(0, size, 256):
         stop = start + 256
@@ -167,7 +327,7 @@
         out_shape=jax.ShapeDtypeStruct(filtered.shape, jnp.bfloat16),
         in_specs=[whole, whole],
         out_specs=whole,
-        scratch_shapes=[pltpu.VMEM(summed_gram.shape, jnp.float32)],
+        scratch_shapes=[pltpu.VMEM((filtered.shape[1],) * 2, jnp.float32)],
         compiler_params=pltpu.CompilerParams(vmem_limit_bytes=48 * 1024 * 1024),
     )(summed_gram, filtered)
 
@@ -203,8 +363,8 @@
         2.0 * (second_product - center * first_step.astype(jnp.float32)) / half_width - start_values
     ).astype(jnp.bfloat16)
     filtered = filtered.reshape(local_rows, orbital_count)
-    summed_gram = lax.psum(
-        jnp.einsum("rc,rd->cd", filtered, filtered, preferred_element_type=jnp.float32), "ex"
+    summed_gram = sum_gram(
+        jnp.einsum("rc,rd->cd", filtered, filtered, preferred_element_type=jnp.float32)
     )
     return orthonormalize(summed_gram, filtered, total_rows)
 

time: 409 us -> 308 us (0.75)
  waiting for transfers between devices: 159 us -> 31.1 us
  Pallas kernels: 113 us -> 208 us
  blocking collectives: 51.3 us -> 0 us
  between operations: 15.1 us -> 1.55 us
    psum x1 -> x0, waiting for transfers between devices: 128 us -> none  [on_device(): lax.psum(jnp.einsum('rc,rd->cd', filtered, filtered, preferred_element_ty...]
    pallas_call x0 -> x2, Pallas kernels: none -> 98.1 us  [the longest x1 63.7 us: sum_gram(): pl.pallas_call(functools.partial(gram_sum_kernel, streams), out_shape=jax...]
    psum x1 -> x0, blocking collectives: 51.3 us -> none  [filter_scalars(): lax.psum((jnp.sum(start_values * product), jnp.sum(start_values * start_v...]
    unnamed x46 -> x36, local copies, waits for them, and re-layouts: 8.66 us -> 5.07 us
  transfers between devices with their start and end apart: 6 -> 5, of which waited for: 3 -> 2; matrix products, arithmetic and copies ran while one was open for 6% -> 8% of each run, Pallas kernels for 0% -> 0%
where the time goes in v2:
time: 308 us
  Pallas kernels  208 us (68%)
  matrix products  42 us (14%)
  waiting for transfers between devices  31.1 us (10%)
  starting transfers between devices  10.5 us (3%)
  local copies, waits for them, and re-layouts  7.87 us (3%)
  other arithmetic  7.05 us (2%)
    pallas_call x1, Pallas kernels, orthonormalize(): pl.pallas_call(functools.partial(orthonormal_kernel, float(row_count)), o...  110 us
    pallas_call x1, Pallas kernels, sum_gram(): pl.pallas_call(functools.partial(gram_sum_kernel, streams), out_shape=jax...  63.7 us
    pallas_call x1, Pallas kernels, sum_scalars(): pl.pallas_call(functools.partial(scalar_sum_kernel, bits), out_shape=jax....  34.4 us
    ppermute x2, waiting for transfers between devices, extended(): lax.ppermute(lax.slice_in_dim(block, block.shape[dim] - width, None, axis...  31 us
    dot_general x2, matrix products, apply_blocks(): jnp.einsum('xyzji,xyzjc->xyzic', next_faces, padded[2:], preferred_elemen...  17.3 us
    dot_general x4, matrix products, apply_blocks(): jnp.einsum('xyzij,xyzjc->xyzic', faces, before, preferred_element_type=jn...  7.03 us
  transfers between devices with their start and end apart: 5, of which 2 were waited for; matrix products, arithmetic and copies ran while one was open for 8% of the time, Pallas kernels for 0%

profile of v2, /device:TPU:0, one launch (start us, length us, event | category | flops | bytes accessed | tf_op | source)
XLA Modules:
  0.0 307.9 jit_solution(9157733559925298986)
XLA Ops:
  0.0 5.4 %collective-permute-start.2 = (bf16[1024,1024]{1,0:T(8,128)(2,1)}, bf16[1024,1024]{1,0:T(8,128)(2,1)S(1)}, u32[]{:S(2)}, u32[]{:S(2)}) collective-permute-start(bf16[1024,1024]{1,0:T(8,128)(2,1)} %param.4), channel_id=1, source_target_pairs={{1,0},{2,1},{3,2},{4,3},{5,4},{6,5},{7,6},{8,7},{9,8},{10,9},{11,1... | collective-permute-start | bytes 6291464 | tf_op jit(solution)/shard_map/ppermute | solution.py:34
  5.4 0.0 collective-permute-start
  5.5 1.4 fusion.16
  6.9 0.0 copy-start.2
  6.9 0.1 fusion.37
  7.0 4.5 %collective-permute-start.1 = (bf16[2,2,256,256]{2,3,1,0:T(8,128)(2,1)S(1)}, bf16[2,2,256,256]{2,3,1,0:T(8,128)(2,1)S(1)}, u32[]{:S(2)}, u32[]{:S(2)}) collective-permute-start(bf16[2,2,256,256]{2,3,1,0:T(8,128)(2,1)S(1)} %bitcast.104), channel_id=1, source_target_pairs={{1,0},{2,1},{3,2},{4,3},{5,4},{6,5},{7,6},{8,7},{9,8},{10,9},{11,1... | collective-permute-start | bytes 1572872 | tf_op jit(solution)/shard_map/ppermute | solution.py:22
  11.6 0.2 fusion.35
  11.8 1.8 multiply_reduce_fusion
  13.6 0.7 fusion.23
  14.3 0.2 fusion.36
  14.5 0.8 fusion.24
  15.3 0.0 copy-start.16
  15.3 0.8 fusion.22
  16.0 0.3 copy-done.16
  16.3 0.7 fusion.41
  17.1 2.7 fusion.21
  19.8 14.1 %collective-permute-done = bf16[1024,1024]{1,0:T(8,128)(2,1)S(1)} collective-permute-done((bf16[1024,1024]{1,0:T(8,128)(2,1)}, bf16[1024,1024]{1,0:T(8,128)(2,1)S(1)}, u32[]{:S(2)}, u32[]{:S(2)}) %collective-permute-start) | collective-permute-done | bytes 2097184 | tf_op jit(solution)/shard_map/ppermute | solution.py:31
  33.9 2.7 fusion.42
  36.6 0.8 copy-done.12
  37.4 1.3 copy-done.14
  38.8 9.4 %fusion = (f32[]{:T(128)}, f32[2,2,256,1024]{3,2,1,0:T(8,128)}) fusion(bf16[2,2,256,1024]{3,2,1,0:T(8,128)(2,1)S(1)} %bitcast.95, f32[2,2,256,1024]{3,2,1,0:T(8,128)} %fusion.21, f32[2,2,256,1024]{3,2,1,0:T(8,128)S(1)} %fusion.22, f32[2,2,256,1024]{3,2,1,0:T(8,128)S(1)} %fusion.23, f32[2,2,256,1024]{3,2,1,0:T(8,128)S(1)} %fusion.24, ...), kind=kOutput, calls=%fused_computation.3 | convolution fusion | flops 546308096 | bytes 34078724 | tf_op jit(solution)/shard_map/xyzji,xyzjc->xyzic/dot_general | solution.py:53
  48.1 1.3 compare_select_fusion
  49.4 0.7 iota.11.own_ref
  50.1 34.4 %shard_map.46 = f32[8,128]{1,0:T(8,128)} custom-call(f32[8,128]{1,0:T(8,128)} %iota.11.own_ref), custom_call_target="tpu_custom_call" | custom-call | tf_op jit(solution)/shard_map/pallas_call | solution.py:174
  84.5 1.3 fusion.40
  87.0 3.1 %fusion.3 = bf16[2,2,256,1024]{3,2,1,0:T(8,128)(2,1)S(1)} fusion(f32[2,2,256,1024]{3,2,1,0:T(8,128)} %get-tuple-element.23, f32[]{:T(128)} %bitcast.16, f32[]{:T(128)} %bitcast.15, bf16[1024,1024]{1,0:T(8,128)(2,1)S(1)} %copy-done.2), kind=kLoop, calls=%fused_computation.6 | loop fusion | flops 5242880 | bytes 8388616 | tf_op jit(solution)/shard_map/convert_element_type | solution.py:360
  90.2 0.3 copy-done.3
  90.5 0.9 fusion.64
  91.4 0.1 collective-permute-start.4
  91.5 0.5 collective-permute-start.3
  91.9 0.2 fusion.33
  92.1 0.2 copy-done.7
  92.3 0.7 fusion.19
  93.1 0.2 fusion.34
  93.2 0.8 copy-done.9
  94.0 0.1 copy-done.11
  94.1 0.7 fusion.17
  94.8 2.8 fusion.20
  97.6 2.7 fusion.18
  100.3 2.7 fusion.44
  103.0 16.9 %collective-permute-done.3 = bf16[1024,1024]{1,0:T(8,128)(2,1)S(1)} collective-permute-done((bf16[1024,1024]{1,0:T(8,128)(2,1)S(1)}, bf16[1024,1024]{1,0:T(8,128)(2,1)S(1)}, u32[]{:S(2)}, u32[]{:S(2)}) %collective-permute-start.3) | collective-permute-done | bytes 2097184 | tf_op jit(solution)/shard_map/ppermute | solution.py:31
  120.0 2.7 fusion.43
  122.7 1.3 copy-done.15
  124.0 8.0 %fusion.4 = bf16[2,2,256,1024]{3,2,1,0:T(8,128)(2,1)S(1)} fusion(bf16[2,2,256,1024]{3,2,1,0:T(8,128)(2,1)S(1)} %fusion.3, f32[2,2,256,1024]{3,2,1,0:T(8,128)S(1)} %fusion.17, f32[2,2,256,1024]{3,2,1,0:T(8,128)} %fusion.18, f32[2,2,256,1024]{3,2,1,0:T(8,128)S(1)} %fusion.19, f32[2,2,256,1024]{3,2,1,0:T(8,128)} %fusion.20, f32[2,2,256,1024]{3,2,1,0:T(8,128)} %fusion.43, ...), kind=kOutput, calls=%fused_computation.7 | convolution fusion | flops 551550976 | bytes 34078728 | tf_op jit(solution)/shard_map/xyzji,xyzjc->xyzic/dot_general | solution.py:53
  131.9 2.4 convolution_bitcast_fusion.gram_ref
  134.4 63.7 %shard_map.47.gram_ref = f32[576,8,128]{2,1,0:T(8,128)S(1)} custom-call(f32[1024,1024]{1,0:T(8,128)S(1)} %convolution_bitcast_fusion.gram_ref), custom_call_target="tpu_custom_call" | custom-call | tf_op jit(solution)/shard_map/pallas_call | solution.py:265
  198.1 0.0 copy-start.1
  198.1 109.8 %shard_map.48 = bf16[1024,1024]{1,0:T(8,128)(2,1)} custom-call(f32[576,8,128]{2,1,0:T(8,128)S(1)} %shard_map.47.gram_ref, bf16[1024,1024]{1,0:T(8,128)(2,1)S(1)} %bitcast.91), custom_call_target="tpu_custom_call" | custom-call | tf_op jit(solution)/shard_map/pallas_call | solution.py:325
  (30 shorter events, 0.1 us)
Async XLA Ops:
  0.0 5.5 %copy-start = (bf16[3,4,256,256]{3,2,1,0:T(8,128)(2,1)S(1)}, bf16[3,4,256,256]{3,2,1,0:T(8,128)(2,1)}, u32[]{:S(2)}) copy-start(bf16[3,4,256,256]{3,2,1,0:T(8,128)(2,1)} %param.6) | copy-start | bytes 4718596
  0.0 37.4 %collective-permute-start.2 = (bf16[1024,1024]{1,0:T(8,128)(2,1)}, bf16[1024,1024]{1,0:T(8,128)(2,1)S(1)}, u32[]{:S(2)}, u32[]{:S(2)}) collective-permute-start(bf16[1024,1024]{1,0:T(8,128)(2,1)} %param.4), channel_id=1, source_target_pairs={{1,0},{2,1},{3,2},{4,3},{5,4},{6,5},{7,6},{8,7},{9,8},{10,9},{11,1... | collective-permute-start | bytes 6291464 | tf_op jit(solution)/shard_map/ppermute | solution.py:34
  5.4 28.5 %collective-permute-start = (bf16[1024,1024]{1,0:T(8,128)(2,1)}, bf16[1024,1024]{1,0:T(8,128)(2,1)S(1)}, u32[]{:S(2)}, u32[]{:S(2)}) collective-permute-start(bf16[1024,1024]{1,0:T(8,128)(2,1)} %param.4), channel_id=1, source_target_pairs={{0,1},{1,2},{2,3},{3,4},{4,5},{5,6},{6,7},{7,8},{8,9},{9,10},{10,1... | collective-permute-start | bytes 6291464 | tf_op jit(solution)/shard_map/ppermute | solution.py:31
  6.9 4.7 %copy-start.2 = (bf16[1024,1024]{1,0:T(8,128)(2,1)S(1)}, bf16[1024,1024]{1,0:T(8,128)(2,1)}, u32[]{:S(2)}) copy-start(bf16[1024,1024]{1,0:T(8,128)(2,1)} %param.4) | copy-start | bytes 6291460
  7.0 26.9 %copy-start.4 = (bf16[1,4,256,256]{2,3,1,0:T(8,128)(2,1)}, bf16[1,4,256,256]{2,3,1,0:T(8,128)(2,1)S(1)}, u32[]{:S(2)}) copy-start(bf16[1,4,256,256]{2,3,1,0:T(8,128)(2,1)S(1)} %get-tuple-element.13) | copy-start | bytes 1572868
  7.0 29.6 %collective-permute-start.1 = (bf16[2,2,256,256]{2,3,1,0:T(8,128)(2,1)S(1)}, bf16[2,2,256,256]{2,3,1,0:T(8,128)(2,1)S(1)}, u32[]{:S(2)}, u32[]{:S(2)}) collective-permute-start(bf16[2,2,256,256]{2,3,1,0:T(8,128)(2,1)S(1)} %bitcast.104), channel_id=1, source_target_pairs={{1,0},{2,1},{3,2},{4,3},{5,4},{6,5},{7,6},{8,7},{9,8},{10,9},{11,1... | collective-permute-start | bytes 1572872 | tf_op jit(solution)/shard_map/ppermute | solution.py:22
  11.6 2.0 copy-start.6
  13.5 3.5 %copy-start.8 = (bf16[1,2,1,256,256]{3,4,2,1,0:T(8,128)(2,1)}, bf16[1,2,1,256,256]{3,4,2,1,0:T(8,128)(2,1)S(1)}, u32[]{:S(2)}) copy-start(bf16[1,2,1,256,256]{3,4,2,1,0:T(8,128)(2,1)S(1)} %get-tuple-element.18) | copy-start | bytes 786436
  13.6 3.5 %copy-start.10 = (bf16[1,2,1,256,256]{3,4,2,1,0:T(8,128)(2,1)}, bf16[1,2,1,256,256]{3,4,2,1,0:T(8,128)(2,1)S(1)}, u32[]{:S(2)}) copy-start(bf16[1,2,1,256,256]{3,4,2,1,0:T(8,128)(2,1)S(1)} %get-tuple-element.19) | copy-start | bytes 786436
  15.3 1.0 copy-start.16
  36.6 0.8 copy-start.12
  37.4 1.3 copy-start.14
  87.0 3.5 %copy-start.3 = (f32[2,2,256,1024]{3,2,1,0:T(8,128)S(1)}, f32[2,2,256,1024]{3,2,1,0:T(8,128)}, u32[]{:S(2)}) copy-start(f32[2,2,256,1024]{3,2,1,0:T(8,128)} %get-tuple-element.23) | copy-start | bytes 12582916
  91.4 1.0 copy-start.7
  91.4 31.3 %collective-permute-start.4 = (bf16[1024,1024]{1,0:T(8,128)(2,1)S(1)}, bf16[1024,1024]{1,0:T(8,128)(2,1)S(1)}, u32[]{:S(2)}, u32[]{:S(2)}) collective-permute-start(bf16[1024,1024]{1,0:T(8,128)(2,1)S(1)} %bitcast.96), channel_id=1, source_target_pairs={{1,0},{2,1},{3,2},{4,3},{5,4},{6,5},{7,6},{8,7},{9,8},{10,9},{11,1... | collective-permute-start | bytes 6291464 | tf_op jit(solution)/shard_map/ppermute | solution.py:34
  91.5 28.5 %collective-permute-start.3 = (bf16[1024,1024]{1,0:T(8,128)(2,1)S(1)}, bf16[1024,1024]{1,0:T(8,128)(2,1)S(1)}, u32[]{:S(2)}, u32[]{:S(2)}) collective-permute-start(bf16[1024,1024]{1,0:T(8,128)(2,1)S(1)} %bitcast.97), channel_id=1, source_target_pairs={{0,1},{1,2},{2,3},{3,4},{4,5},{5,6},{6,7},{7,8},{8,9},{9,10},{10,1... | collective-permute-start | bytes 6291464 | tf_op jit(solution)/shard_map/ppermute | solution.py:31
  93.0 1.0 copy-start.9
  93.1 1.0 copy-start.11
  97.6 2.7 copy-start.17
  100.3 19.6 %copy-start.5 = (bf16[1,4,256,256]{2,3,1,0:T(8,128)(2,1)S(1)}, bf16[1,4,256,256]{2,3,1,0:T(8,128)(2,1)}, u32[]{:S(2)}) copy-start(bf16[1,4,256,256]{2,3,1,0:T(8,128)(2,1)} %copy-done.4) | copy-start | bytes 1572868
  119.9 4.0 %copy-start.13 = (bf16[2,2,256,256]{2,3,1,0:T(8,128)(2,1)S(1)}, bf16[2,2,256,256]{2,3,1,0:T(8,128)(2,1)}, u32[]{:S(2)}) copy-start(bf16[2,2,256,256]{2,3,1,0:T(8,128)(2,1)} %copy-done.12) | copy-start | bytes 1572868
  122.7 1.3 copy-start.15
  198.1 109.8 %copy-start.1 = (bf16[3,4,256,256]{3,2,1,0:T(8,128)(2,1)S(1)}, bf16[3,4,256,256]{3,2,1,0:T(8,128)(2,1)}, u32[]{:S(2)}) copy-start(bf16[3,4,256,256]{3,2,1,0:T(8,128)(2,1)} %param.6) | copy-start | bytes 4718596

commit v3 on v2

--- a/solution.py
+++ b/solution.py
@@ -93,28 +93,30 @@
     sub = lax.broadcasted_iota(jnp.int32, (8, 1), 0)
 
     def group(step, state):
-        state = list(state)
+        head = state[0]
+        columns = [jnp.broadcast_to(head[:, j : j + 1], (8, BLOCK)) for j in range(8)]
+        rows = jnp.where(lane < 8, jnp.where(lane == sub, 1.0, 0.0), head)
         for j in range(8):
-            here = lane == j
-            head = state[0]
-            pivot = head[j : j + 1, j : j + 1]
-            scale = lax.rsqrt(pivot)
-            row = jnp.where(here, 1.0, head[j : j + 1, :])
-            scaled = row * scale
-            used = scaled * scale
-            for t in range(tiles):
-                column = state[t][:, j : j + 1]
-                if t == 0:
-                    column = jnp.where(sub > j, column, 0.0)
-                    kept = jnp.where(here & (sub > j), 0.0, state[t])
-                    new = kept - column * used
-                    state[t] = jnp.where(sub == j, scaled, new)
-                else:
-                    live = t < tiles - step
-                    new = jnp.where(here, 0.0, state[t]) - column * used
-                    state[t] = jnp.where(live, new, state[t])
-        state = [pltpu.roll(x, BLOCK - 8, 1) for x in state]
-        return tuple(state[1:] + state[:1])
+            factor = jnp.where(sub > j, columns[j] * (1.0 / columns[j][j : j + 1, :]), 0.0)
+            for k in range(j + 1, 8):
+                columns[k] = columns[k] - factor * columns[k][j : j + 1, :]
+            rows = rows - factor * rows[j : j + 1, :]
+        pivots = columns[0]
+        for j in range(1, 8):
+            pivots = jnp.where(sub == j, columns[j], pivots)
+        inverse = 1.0 / pivots
+        solved = rows * inverse
+        for j in range(7, 0, -1):
+            factor = jnp.where(sub < j, columns[j] * inverse, 0.0)
+            solved = solved - factor * solved[j : j + 1, :]
+        result = []
+        for t in range(1, tiles):
+            new = jnp.where(lane < 8, 0.0, state[t])
+            for j in range(8):
+                new = new - state[t][:, j : j + 1] * solved[j : j + 1, :]
+            result.append(jnp.where(t < tiles - step, new, state[t]))
+        result.append(rows * lax.rsqrt(pivots))
+        return tuple(pltpu.roll(x, BLOCK - 8, 1) for x in result)
 
     state = tuple(block[8 * t : 8 * t + 8, :] for t in range(tiles))
     state = lax.fori_loop(0, tiles, group, state)

time: 308 us -> 259 us (0.84)
  Pallas kernels: 208 us -> 158 us
    pallas_call x1, Pallas kernels: 110 us -> 60.4 us  [orthonormalize(): pl.pallas_call(functools.partial(orthonormal_kernel, float(row_count)), o...]
  transfers between devices with their start and end apart: 5 -> 5, of which waited for: 2 -> 2; matrix products, arithmetic and copies ran while one was open for 8% -> 10% of each run, Pallas kernels for 0% -> 0%
where the time goes in v3:
time: 259 us; the launch traced here: 258 us
  Pallas kernels  158 us (61%)
  matrix products  42 us (16%)
  waiting for transfers between devices  31.1 us (12%)
  starting transfers between devices  10.5 us (4%)
  local copies, waits for them, and re-layouts  7.87 us (3%)
  other arithmetic  7.05 us (3%)
    pallas_call x1, Pallas kernels, sum_gram(): pl.pallas_call(functools.partial(gram_sum_kernel, streams), out_shape=jax...  63.7 us
    pallas_call x1, Pallas kernels, orthonormalize(): pl.pallas_call(functools.partial(orthonormal_kernel, float(row_count)), o...  60.4 us
    pallas_call x1, Pallas kernels, sum_scalars(): pl.pallas_call(functools.partial(scalar_sum_kernel, bits), out_shape=jax....  34.4 us
    ppermute x2, waiting for transfers between devices, extended(): lax.ppermute(lax.slice_in_dim(block, block.shape[dim] - width, None, axis...  31 us
    dot_general x2, matrix products, apply_blocks(): jnp.einsum('xyzji,xyzjc->xyzic', next_faces, padded[2:], preferred_elemen...  17.3 us
    dot_general x4, matrix products, apply_blocks(): jnp.einsum('xyzij,xyzjc->xyzic', faces, before, preferred_element_type=jn...  7.03 us
    ppermute x2, starting transfers between devices, extended(): lax.ppermute(lax.slice_in_dim(block, 0, width, axis=dim), axis, backward)  5.5 us
    dot_general x2, matrix products, apply_blocks(): jnp.einsum('xyzij,xyzjc->xyzic', coupled[0], padded[:-2], preferred_eleme...  5.4 us
  transfers between devices with their start and end apart: 5, of which 2 were waited for; matrix products, arithmetic and copies ran while one was open for 10% of the time, Pallas kernels for 0%

profile of v3, /device:TPU:0, one launch (start us, length us, event | category | flops | bytes accessed | tf_op | source)
XLA Modules:
  0.0 258.4 jit_solution(12110024118924859705)
XLA Ops:
  0.0 5.4 %collective-permute-start.2 = (bf16[1024,1024]{1,0:T(8,128)(2,1)}, bf16[1024,1024]{1,0:T(8,128)(2,1)S(1)}, u32[]{:S(2)}, u32[]{:S(2)}) collective-permute-start(bf16[1024,1024]{1,0:T(8,128)(2,1)} %param.4), channel_id=1, source_target_pairs={{1,0},{2,1},{3,2},{4,3},{5,4},{6,5},{7,6},{8,7},{9,8},{10,9},{11,1... | collective-permute-start | bytes 6291464 | tf_op jit(solution)/shard_map/ppermute | solution.py:34
  5.5 1.4 fusion.16
  6.9 0.0 copy-start.2
  6.9 0.1 fusion.37
  7.0 4.5 %collective-permute-start.1 = (bf16[2,2,256,256]{2,3,1,0:T(8,128)(2,1)S(1)}, bf16[2,2,256,256]{2,3,1,0:T(8,128)(2,1)S(1)}, u32[]{:S(2)}, u32[]{:S(2)}) collective-permute-start(bf16[2,2,256,256]{2,3,1,0:T(8,128)(2,1)S(1)} %bitcast.104), channel_id=1, source_target_pairs={{1,0},{2,1},{3,2},{4,3},{5,4},{6,5},{7,6},{8,7},{9,8},{10,9},{11,1... | collective-permute-start | bytes 1572872 | tf_op jit(solution)/shard_map/ppermute | solution.py:22
  11.6 0.2 fusion.35
  11.8 1.8 multiply_reduce_fusion
  13.6 0.7 fusion.23
  14.3 0.2 fusion.36
  14.5 0.8 fusion.24
  15.3 0.0 copy-start.16
  15.3 0.8 fusion.22
  16.0 0.3 copy-done.16
  16.3 0.7 fusion.41
  17.1 2.7 %fusion.21 = f32[2,2,256,1024]{3,2,1,0:T(8,128)} fusion(bf16[1,2,1,256,1024]{4,3,2,1,0:T(8,128)(2,1)S(1)} %get-tuple-element.12, bf16[1,2,1,256,1024]{4,3,2,1,0:T(8,128)(2,1)S(1)} %get-tuple-element.11, bf16[1,2,1,256,256]{3,4,2,1,0:T(8,128)(2,1)S(1)} %get-tuple-element.19, bf16[1,2,1,256,256]{3,4,2,1,0:T(8,128)(2,1)S(1)} %get-tuple-element.18), kind=kOutput, calls=%fused_computation.33 | convolution fusion | flops 538181632 | bytes 6815744 | tf_op jit(solution)/shard_map/xyzji,xyzjc->xyzic/dot_general | solution.py:64
  19.8 14.1 %collective-permute-done = bf16[1024,1024]{1,0:T(8,128)(2,1)S(1)} collective-permute-done((bf16[1024,1024]{1,0:T(8,128)(2,1)}, bf16[1024,1024]{1,0:T(8,128)(2,1)S(1)}, u32[]{:S(2)}, u32[]{:S(2)}) %collective-permute-start) | collective-permute-done | bytes 2097184 | tf_op jit(solution)/shard_map/ppermute | solution.py:31
  33.9 2.7 %fusion.42 = f32[2,2,256,1024]{3,2,1,0:T(8,128)} fusion(bf16[2,2,256,256]{2,3,1,0:T(8,128)(2,1)S(1)} %bitcast.105, bf16[2,2,256,1024]{3,2,1,0:T(8,128)(2,1)S(1)} %bitcast.109), kind=kOutput, calls=%fused_computation.57 | convolution fusion | flops 536870912 | bytes 6815744 | tf_op jit(solution)/shard_map/xyzij,xyzjc->xyzic/dot_general | solution.py:50
  36.6 0.0 collective-permute-done.1
  36.6 0.8 copy-done.12
  37.4 1.3 copy-done.14
  38.8 9.4 %fusion = (f32[]{:T(128)}, f32[2,2,256,1024]{3,2,1,0:T(8,128)}) fusion(bf16[2,2,256,1024]{3,2,1,0:T(8,128)(2,1)S(1)} %bitcast.95, f32[2,2,256,1024]{3,2,1,0:T(8,128)} %fusion.21, f32[2,2,256,1024]{3,2,1,0:T(8,128)S(1)} %fusion.22, f32[2,2,256,1024]{3,2,1,0:T(8,128)S(1)} %fusion.23, f32[2,2,256,1024]{3,2,1,0:T(8,128)S(1)} %fusion.24, ...), kind=kOutput, calls=%fused_computation.3 | convolution fusion | flops 546308096 | bytes 34078724 | tf_op jit(solution)/shard_map/xyzji,xyzjc->xyzic/dot_general | solution.py:53
  48.1 1.3 compare_select_fusion
  49.4 0.7 iota.11.own_ref
  50.1 34.4 %shard_map.46 = f32[8,128]{1,0:T(8,128)} custom-call(f32[8,128]{1,0:T(8,128)} %iota.11.own_ref), custom_call_target="tpu_custom_call" | custom-call | tf_op jit(solution)/shard_map/pallas_call | solution.py:176
  84.5 1.3 fusion.40
  87.0 3.1 %fusion.3 = bf16[2,2,256,1024]{3,2,1,0:T(8,128)(2,1)S(1)} fusion(f32[2,2,256,1024]{3,2,1,0:T(8,128)} %get-tuple-element.23, f32[]{:T(128)} %bitcast.16, f32[]{:T(128)} %bitcast.15, bf16[1024,1024]{1,0:T(8,128)(2,1)S(1)} %copy-done.2), kind=kLoop, calls=%fused_computation.6 | loop fusion | flops 5242880 | bytes 8388616 | tf_op jit(solution)/shard_map/convert_element_type | solution.py:362
  90.2 0.3 copy-done.3
  90.5 0.9 fusion.64
  91.4 0.1 collective-permute-start.4
  91.5 0.5 collective-permute-start.3
  91.9 0.2 fusion.33
  92.1 0.2 copy-done.7
  92.3 0.7 fusion.19
  93.1 0.2 fusion.34
  93.2 0.8 copy-done.9
  94.0 0.1 copy-done.11
  94.1 0.7 fusion.17
  94.8 2.8 %fusion.20 = f32[2,2,256,1024]{3,2,1,0:T(8,128)} fusion(bf16[2,2,256,256]{2,3,1,0:T(8,128)(2,1)S(1)} %bitcast.103, bf16[1,1,2,256,1024]{4,3,2,1,0:T(8,128)(2,1)S(1)} %get-tuple-element.6, bf16[1,1,2,256,1024]{4,3,2,1,0:T(8,128)(2,1)S(1)} %get-tuple-element.5), kind=kOutput, calls=%fused_computation.32 | convolution fusion | flops 537919488 | bytes 6815744 | tf_op jit(solution)/shard_map/xyzij,xyzjc->xyzic/dot_general | solution.py:61
  97.6 2.7 %fusion.18 = f32[2,2,256,1024]{3,2,1,0:T(8,128)} fusion(bf16[2,2,256,256]{2,3,1,0:T(8,128)(2,1)S(1)} %bitcast.100, bf16[1,2,1,256,1024]{4,3,2,1,0:T(8,128)(2,1)S(1)} %get-tuple-element.8, bf16[1,2,1,256,1024]{4,3,2,1,0:T(8,128)(2,1)S(1)} %get-tuple-element.7), kind=kOutput, calls=%fused_computation.30 | convolution fusion | flops 537919488 | bytes 6815744 | tf_op jit(solution)/shard_map/xyzij,xyzjc->xyzic/dot_general | solution.py:61
  100.3 2.7 %fusion.44 = f32[2,2,1024,256]{2,3,1,0:T(8,128)} fusion(bf16[2,2,256,256]{3,2,1,0:T(8,128)(2,1)S(1)} %bitcast.112, bf16[2,2,256,1024]{3,2,1,0:T(8,128)(2,1)S(1)} %fusion.3), kind=kOutput, calls=%fused_computation.59 | convolution fusion | flops 536870912 | bytes 6815744 | tf_op jit(solution)/shard_map/xyzij,xyzjc->xyzic/dot_general | solution.py:49
  103.0 16.9 %collective-permute-done.3 = bf16[1024,1024]{1,0:T(8,128)(2,1)S(1)} collective-permute-done((bf16[1024,1024]{1,0:T(8,128)(2,1)S(1)}, bf16[1024,1024]{1,0:T(8,128)(2,1)S(1)}, u32[]{:S(2)}, u32[]{:S(2)}) %collective-permute-start.3) | collective-permute-done | bytes 2097184 | tf_op jit(solution)/shard_map/ppermute | solution.py:31
  120.0 2.7 %fusion.43 = f32[2,2,256,1024]{3,2,1,0:T(8,128)} fusion(bf16[2,2,256,256]{2,3,1,0:T(8,128)(2,1)S(1)} %bitcast.106, bf16[2,2,256,1024]{3,2,1,0:T(8,128)(2,1)S(1)} %bitcast.110), kind=kOutput, calls=%fused_computation.58 | convolution fusion | flops 536870912 | bytes 6815744 | tf_op jit(solution)/shard_map/xyzij,xyzjc->xyzic/dot_general | solution.py:50
  122.7 1.3 copy-done.15
  124.0 8.0 %fusion.4 = bf16[2,2,256,1024]{3,2,1,0:T(8,128)(2,1)S(1)} fusion(bf16[2,2,256,1024]{3,2,1,0:T(8,128)(2,1)S(1)} %fusion.3, f32[2,2,256,1024]{3,2,1,0:T(8,128)S(1)} %fusion.17, f32[2,2,256,1024]{3,2,1,0:T(8,128)} %fusion.18, f32[2,2,256,1024]{3,2,1,0:T(8,128)S(1)} %fusion.19, f32[2,2,256,1024]{3,2,1,0:T(8,128)} %fusion.20, f32[2,2,256,1024]{3,2,1,0:T(8,128)} %fusion.43, ...), kind=kOutput, calls=%fused_computation.7 | convolution fusion | flops 551550976 | bytes 34078728 | tf_op jit(solution)/shard_map/xyzji,xyzjc->xyzic/dot_general | solution.py:53
  131.9 2.4 convolution_bitcast_fusion.gram_ref
  134.4 63.7 %shard_map.47.gram_ref = f32[576,8,128]{2,1,0:T(8,128)S(1)} custom-call(f32[1024,1024]{1,0:T(8,128)S(1)} %convolution_bitcast_fusion.gram_ref), custom_call_target="tpu_custom_call" | custom-call | tf_op jit(solution)/shard_map/pallas_call | solution.py:267
  198.1 0.0 copy-start.1
  198.1 60.4 %shard_map.48 = bf16[1024,1024]{1,0:T(8,128)(2,1)} custom-call(f32[576,8,128]{2,1,0:T(8,128)S(1)} %shard_map.47.gram_ref, bf16[1024,1024]{1,0:T(8,128)(2,1)S(1)} %bitcast.91), custom_call_target="tpu_custom_call" | custom-call | tf_op jit(solution)/shard_map/pallas_call | solution.py:327
  (30 shorter events, 0.1 us)
Async XLA Ops:
  0.0 5.5 %copy-start = (bf16[3,4,256,256]{3,2,1,0:T(8,128)(2,1)S(1)}, bf16[3,4,256,256]{3,2,1,0:T(8,128)(2,1)}, u32[]{:S(2)}) copy-start(bf16[3,4,256,256]{3,2,1,0:T(8,128)(2,1)} %param.6) | copy-start | bytes 4718596
  0.0 37.4 %collective-permute-start.2 = (bf16[1024,1024]{1,0:T(8,128)(2,1)}, bf16[1024,1024]{1,0:T(8,128)(2,1)S(1)}, u32[]{:S(2)}, u32[]{:S(2)}) collective-permute-start(bf16[1024,1024]{1,0:T(8,128)(2,1)} %param.4), channel_id=1, source_target_pairs={{1,0},{2,1},{3,2},{4,3},{5,4},{6,5},{7,6},{8,7},{9,8},{10,9},{11,1... | collective-permute-start | bytes 6291464 | tf_op jit(solution)/shard_map/ppermute | solution.py:34
  5.4 28.5 %collective-permute-start = (bf16[1024,1024]{1,0:T(8,128)(2,1)}, bf16[1024,1024]{1,0:T(8,128)(2,1)S(1)}, u32[]{:S(2)}, u32[]{:S(2)}) collective-permute-start(bf16[1024,1024]{1,0:T(8,128)(2,1)} %param.4), channel_id=1, source_target_pairs={{0,1},{1,2},{2,3},{3,4},{4,5},{5,6},{6,7},{7,8},{8,9},{9,10},{10,1... | collective-permute-start | bytes 6291464 | tf_op jit(solution)/shard_map/ppermute | solution.py:31
  6.9 4.7 %copy-start.2 = (bf16[1024,1024]{1,0:T(8,128)(2,1)S(1)}, bf16[1024,1024]{1,0:T(8,128)(2,1)}, u32[]{:S(2)}) copy-start(bf16[1024,1024]{1,0:T(8,128)(2,1)} %param.4) | copy-start | bytes 6291460
  7.0 26.9 %copy-start.4 = (bf16[1,4,256,256]{2,3,1,0:T(8,128)(2,1)}, bf16[1,4,256,256]{2,3,1,0:T(8,128)(2,1)S(1)}, u32[]{:S(2)}) copy-start(bf16[1,4,256,256]{2,3,1,0:T(8,128)(2,1)S(1)} %get-tuple-element.13) | copy-start | bytes 1572868
  7.0 29.6 %collective-permute-start.1 = (bf16[2,2,256,256]{2,3,1,0:T(8,128)(2,1)S(1)}, bf16[2,2,256,256]{2,3,1,0:T(8,128)(2,1)S(1)}, u32[]{:S(2)}, u32[]{:S(2)}) collective-permute-start(bf16[2,2,256,256]{2,3,1,0:T(8,128)(2,1)S(1)} %bitcast.104), channel_id=1, source_target_pairs={{1,0},{2,1},{3,2},{4,3},{5,4},{6,5},{7,6},{8,7},{9,8},{10,9},{11,1... | collective-permute-start | bytes 1572872 | tf_op jit(solution)/shard_map/ppermute | solution.py:22
  11.6 2.0 copy-start.6
  13.5 3.5 %copy-start.8 = (bf16[1,2,1,256,256]{3,4,2,1,0:T(8,128)(2,1)}, bf16[1,2,1,256,256]{3,4,2,1,0:T(8,128)(2,1)S(1)}, u32[]{:S(2)}) copy-start(bf16[1,2,1,256,256]{3,4,2,1,0:T(8,128)(2,1)S(1)} %get-tuple-element.18) | copy-start | bytes 786436
  13.6 3.5 %copy-start.10 = (bf16[1,2,1,256,256]{3,4,2,1,0:T(8,128)(2,1)}, bf16[1,2,1,256,256]{3,4,2,1,0:T(8,128)(2,1)S(1)}, u32[]{:S(2)}) copy-start(bf16[1,2,1,256,256]{3,4,2,1,0:T(8,128)(2,1)S(1)} %get-tuple-element.19) | copy-start | bytes 786436
  15.3 1.0 copy-start.16
  36.6 0.8 copy-start.12
  37.4 1.3 copy-start.14
  87.0 3.5 %copy-start.3 = (f32[2,2,256,1024]{3,2,1,0:T(8,128)S(1)}, f32[2,2,256,1024]{3,2,1,0:T(8,128)}, u32[]{:S(2)}) copy-start(f32[2,2,256,1024]{3,2,1,0:T(8,128)} %get-tuple-element.23) | copy-start | bytes 12582916
  91.4 1.0 copy-start.7
  91.4 31.3 %collective-permute-start.4 = (bf16[1024,1024]{1,0:T(8,128)(2,1)S(1)}, bf16[1024,1024]{1,0:T(8,128)(2,1)S(1)}, u32[]{:S(2)}, u32[]{:S(2)}) collective-permute-start(bf16[1024,1024]{1,0:T(8,128)(2,1)S(1)} %bitcast.96), channel_id=1, source_target_pairs={{1,0},{2,1},{3,2},{4,3},{5,4},{6,5},{7,6},{8,7},{9,8},{10,9},{11,1... | collective-permute-start | bytes 6291464 | tf_op jit(solution)/shard_map/ppermute | solution.py:34
  91.5 28.5 %collective-permute-start.3 = (bf16[1024,1024]{1,0:T(8,128)(2,1)S(1)}, bf16[1024,1024]{1,0:T(8,128)(2,1)S(1)}, u32[]{:S(2)}, u32[]{:S(2)}) collective-permute-start(bf16[1024,1024]{1,0:T(8,128)(2,1)S(1)} %bitcast.97), channel_id=1, source_target_pairs={{0,1},{1,2},{2,3},{3,4},{4,5},{5,6},{6,7},{7,8},{8,9},{9,10},{10,1... | collective-permute-start | bytes 6291464 | tf_op jit(solution)/shard_map/ppermute | solution.py:31
  93.0 1.0 copy-start.9
  93.1 1.0 copy-start.11
  97.6 2.7 %copy-start.17 = (bf16[4,256,256]{2,1,0:T(8,128)(2,1)S(1)}, bf16[4,256,256]{2,1,0:T(8,128)(2,1)}, u32[]{:S(2)}) copy-start(bf16[4,256,256]{2,1,0:T(8,128)(2,1)} %param.5) | copy-start | bytes 1572868
  100.3 19.6 %copy-start.5 = (bf16[1,4,256,256]{2,3,1,0:T(8,128)(2,1)S(1)}, bf16[1,4,256,256]{2,3,1,0:T(8,128)(2,1)}, u32[]{:S(2)}) copy-start(bf16[1,4,256,256]{2,3,1,0:T(8,128)(2,1)} %copy-done.4) | copy-start | bytes 1572868
  119.9 4.0 %copy-start.13 = (bf16[2,2,256,256]{2,3,1,0:T(8,128)(2,1)S(1)}, bf16[2,2,256,256]{2,3,1,0:T(8,128)(2,1)}, u32[]{:S(2)}) copy-start(bf16[2,2,256,256]{2,3,1,0:T(8,128)(2,1)} %copy-done.12) | copy-start | bytes 1572868
  122.7 1.3 copy-start.15
  198.1 60.4 %copy-start.1 = (bf16[3,4,256,256]{3,2,1,0:T(8,128)(2,1)S(1)}, bf16[3,4,256,256]{3,2,1,0:T(8,128)(2,1)}, u32[]{:S(2)}) copy-start(bf16[3,4,256,256]{3,2,1,0:T(8,128)(2,1)} %param.6) | copy-start | bytes 4718596

commit v4 on v3

--- a/solution.py
+++ b/solution.py
@@ -10,6 +10,7 @@
 EY = 2
 EZ = 2
 BLOCK = 128
+CHUNKS = 2
 
 
 spectrum_top = 14.0
@@ -22,18 +23,13 @@
     return lax.ppermute(block, axis, route)
 
 
-def extended(block, sides, width):
-    for axis, dim in sides:
-        count = lax.axis_size(axis)
-        forward = [(i, i + 1) for i in range(count - 1)]
-        forward.append((count - 1, 0))
-        backward = [(target, source) for source, target in forward]
-        low = lax.ppermute(
-            lax.slice_in_dim(block, block.shape[dim] - width, None, axis=dim), axis, forward
-        )
-        high = lax.ppermute(lax.slice_in_dim(block, 0, width, axis=dim), axis, backward)
-        block = jnp.concatenate([low, block, high], axis=dim)
-    return block
+def halo(block, width):
+    count = lax.axis_size("ex")
+    forward = [(i, (i + 1) % count) for i in range(count)]
+    backward = [(target, source) for source, target in forward]
+    low = lax.ppermute(block[block.shape[0] - width :], "ex", forward)
+    high = lax.ppermute(block[:width], "ex", backward)
+    return low, high
 
 
 def build_coupled(face_couplings, face_order):
@@ -67,10 +63,8 @@
     return total
 
 
-def filter_scalars(start_values, product, total_count):
-    energy, weight = sum_scalars(
-        jnp.sum(start_values * product), jnp.sum(start_values * start_values)
-    )
+def filter_scalars(energy, weight, total_count):
+    energy, weight = sum_scalars(energy, weight)
     cut_level = energy / total_count / (weight / total_count + mean_epsilon)
     return ((spectrum_top + cut_level) * 0.5, (spectrum_top - cut_level) * 0.5)
 
@@ -348,23 +342,42 @@
     blocks = element_blocks.reshape(layers, EY, EZ, basis_size, basis_size)
     beyond = from_behind(coupled[0, 0], "ex", -1)
     next_faces = jnp.concatenate([coupled[0, 1:], beyond[None]], axis=0)
-    start_blocks = orbitals.reshape(layers, EY, EZ, basis_size, orbital_count)
-    start_values = start_blocks.astype(jnp.float32)
-
-    def neighbour_product(values):
-        flat_values = values.reshape(local_rows, orbital_count)
-        padded = extended(flat_values, (("ex", 0),), slab_rows)
-        padded = padded.reshape(layers + 2, EY, EZ, basis_size, orbital_count)
-        return apply_blocks(blocks, coupled, next_faces, padded)
-
-    product = neighbour_product(start_blocks)
-    center, half_width = filter_scalars(start_values, product, total_count)
-    first_step = ((product - center * start_values) / half_width).astype(jnp.bfloat16)
-    second_product = neighbour_product(first_step)
-    filtered = (
-        2.0 * (second_product - center * first_step.astype(jnp.float32)) / half_width - start_values
-    ).astype(jnp.bfloat16)
-    filtered = filtered.reshape(local_rows, orbital_count)
+    chunk = orbital_count // CHUNKS
+
+    def neighbour_product(values, sides):
+        padded = jnp.concatenate([sides[0], values, sides[1]], axis=0)
+        padded = padded.reshape(layers + 2, EY, EZ, basis_size, chunk)
+        return apply_blocks(blocks, coupled, next_faces, padded).reshape(local_rows, chunk)
+
+    starts = [orbitals[:, i * chunk : (i + 1) * chunk] for i in range(CHUNKS)]
+    sides = [halo(starts[0], slab_rows)]
+    for i in range(1, CHUNKS):
+        sent, sides[i - 1] = lax.optimization_barrier((starts[i], sides[i - 1]))
+        sides.append(halo(sent, slab_rows))
+    products = [neighbour_product(*pair) for pair in zip(starts, sides)]
+    energy = sum(jnp.sum(v.astype(jnp.float32) * p) for v, p in zip(starts, products))
+    weight = jnp.sum(jnp.square(orbitals.astype(jnp.float32)))
+    rounded = [p.astype(jnp.bfloat16) for p in products]
+    before = sides[CHUNKS - 1]
+    second_sides = []
+    for i in range(CHUNKS):
+        if i > 0:
+            sent, before = lax.optimization_barrier((rounded[i], before))
+            second_sides[i - 1] = before
+        else:
+            sent = rounded[i]
+        before = halo(sent, slab_rows)
+        second_sides.append(before)
+    energy, weight, second_sides[0] = lax.optimization_barrier((energy, weight, second_sides[0]))
+    center, half_width = filter_scalars(energy, weight, total_count)
+    parts = []
+    for value, product, narrow, beside in zip(starts, products, rounded, second_sides):
+        wide = value.astype(jnp.float32)
+        twice = neighbour_product(narrow, beside)
+        second = (twice - center * narrow.astype(jnp.float32)) / half_width
+        first = (product - center * wide) / half_width
+        parts.append((2.0 * (second - center * first) / half_width - wide).astype(jnp.bfloat16))
+    filtered = jnp.concatenate(parts, axis=1)
     summed_gram = sum_gram(
         jnp.einsum("rc,rd->cd", filtered, filtered, preferred_element_type=jnp.float32)
     )

time: 259 us -> 246 us (0.950)
  starting transfers between devices: 10.5 us -> 60.2 us
  Pallas kernels: 158 us -> 127 us
  waiting for transfers between devices: 31.1 us -> 2.5 us
  matrix products: 42 us -> 36.5 us
    ppermute x4 -> x8, starting transfers between devices: 6 us -> 59.4 us  [the longest x4 54.4 us: halo(): low = lax.ppermute(block[block.shape[0] - width:], 'ex', forward)]
    ppermute x4 -> x8, waiting for transfers between devices: 31.1 us -> 2.5 us  [the longest x4 2.49 us: halo(): low = lax.ppermute(block[block.shape[0] - width:], 'ex', forward)]
    pallas_call x1, Pallas kernels: 34.4 us -> 16 us  [sum_scalars(): pl.pallas_call(functools.partial(scalar_sum_kernel, bits), out_shape=jax....]
    pallas_call x1, Pallas kernels: 63.7 us -> 50.3 us  [sum_gram(): pl.pallas_call(functools.partial(gram_sum_kernel, streams), out_shape=jax...]
    dot_general x2 -> x4, matrix products: 17.3 us -> 5.86 us  [apply_blocks(): jnp.einsum('xyzji,xyzjc->xyzic', next_faces, padded[2:], preferred_elemen...]
    dot_general x4 -> x8, matrix products: 4.91 us -> 9.06 us  [apply_blocks(): jnp.einsum('xyzji,xyzjc->xyzic', faces_after, after, preferred_element_ty...]
    ppermute x1, starting transfers between devices: 4.49 us -> 0.73 us  [from_behind(): return lax.ppermute(block, axis, route)]
    dot_general x4 -> x8, matrix products: 7.03 us -> 9.27 us  [apply_blocks(): jnp.einsum('xyzij,xyzjc->xyzic', faces, before, preferred_element_type=jn...]
  transfers between devices with their start and end apart: 5 -> 9, of which waited for: 2 -> 1; matrix products, arithmetic and copies ran while one was open for 10% -> 17% of each run, Pallas kernels for 0% -> 7%
where the time goes in v4:
time: 246 us
  Pallas kernels  127 us (52%)
  starting transfers between devices  60.2 us (24%)
  matrix products  36.5 us (15%)
  other arithmetic  8.91 us (4%)
  local copies, waits for them, and re-layouts  8.08 us (3%)
  between operations  3.21 us (1%)
  waiting for transfers between devices  2.5 us (1%)
    pallas_call x1, Pallas kernels, orthonormalize(): pl.pallas_call(functools.partial(orthonormal_kernel, float(row_count)), o...  60.4 us
    ppermute x4, starting transfers between devices, halo(): low = lax.ppermute(block[block.shape[0] - width:], 'ex', forward)  54.4 us
    pallas_call x1, Pallas kernels, sum_gram(): pl.pallas_call(functools.partial(gram_sum_kernel, streams), out_shape=jax...  50.3 us
    pallas_call x1, Pallas kernels, sum_scalars(): pl.pallas_call(functools.partial(scalar_sum_kernel, bits), out_shape=jax....  16 us
    dot_general x8, matrix products, apply_blocks(): jnp.einsum('xyzij,xyzjc->xyzic', faces, before, preferred_element_type=jn...  9.27 us
    dot_general x8, matrix products, apply_blocks(): jnp.einsum('xyzji,xyzjc->xyzic', faces_after, after, preferred_element_ty...  9.06 us
    dot_general x4, matrix products, apply_blocks(): jnp.einsum('xyzji,xyzjc->xyzic', next_faces, padded[2:], preferred_elemen...  5.86 us
    ppermute x4, starting transfers between devices, halo(): high = lax.ppermute(block[:width], 'ex', backward)  5.07 us
  transfers between devices with their start and end apart: 9, of which 1 were waited for; matrix products, arithmetic and copies ran while one was open for 17% of the time, Pallas kernels for 7%

profile of v4, /device:TPU:0, one launch (start us, length us, event | category | flops | bytes accessed | tf_op | source)
XLA Modules:
  0.0 246.1 jit_solution(17965750286180768703)
XLA Ops:
  0.0 1.8 fusion.69
  1.8 0.5 collective-permute-start
  2.3 5.1 %collective-permute-start.1 = (bf16[1024,512]{1,0:T(8,128)(2,1)S(1)}, bf16[1024,512]{1,0:T(8,128)(2,1)S(1)}, u32[]{:S(2)}, u32[]{:S(2)}) collective-permute-start(bf16[1024,512]{1,0:T(8,128)(2,1)S(1)} %get-tuple-element.33), channel_id=1, source_target_pairs={{1,0},{2,1},{3,2},{4,3},{5,4},{6,5},{7,6},{8,7},{9,8},{10,9},{11,1... | collective-permute-start | bytes 3145736 | tf_op jit(solution)/shard_map/ppermute | solution.py:31
  7.4 0.7 fusion.31
  8.2 0.7 collective-permute-start.2
  9.3 0.5 fusion.43
  9.8 0.4 fusion.42
  10.2 0.4 fusion.46
  10.7 0.5 fusion.47
  11.2 0.5 fusion.41
  11.7 0.5 fusion.45
  12.2 0.4 fusion.40
  13.1 0.6 copy-done.6
  14.6 1.1 copy-done.4
  15.7 1.7 multiply_reduce_fusion
  17.4 2.5 %collective-permute-done = bf16[1024,512]{1,0:T(8,128)(2,1)S(1)} collective-permute-done((bf16[1024,512]{1,0:T(8,128)(2,1)S(1)}, bf16[1024,512]{1,0:T(8,128)(2,1)S(1)}, u32[]{:S(2)}, u32[]{:S(2)}) %collective-permute-start) | collective-permute-done | bytes 1048608 | tf_op jit(solution)/shard_map/ppermute | solution.py:30
  19.9 21.7 %collective-permute-start.3 = (bf16[1024,512]{1,0:T(8,128)(2,1)S(1)}, bf16[1024,512]{1,0:T(8,128)(2,1)S(1)}, u32[]{:S(2)}, u32[]{:S(2)}) collective-permute-start(bf16[1024,512]{1,0:T(8,128)(2,1)S(1)} %get-tuple-element.17), channel_id=1, source_target_pairs={{0,1},{1,2},{2,3},{3,4},{4,5},{5,6},{6,7},{7,8},{8,9},{9,10},{10,1... | collective-permute-start | bytes 3145736 | tf_op jit(solution)/shard_map/ppermute | solution.py:30
  41.6 0.5 fusion.83
  42.1 0.8 add_add_fusion.1
  43.2 5.2 %collective-permute-start.5 = (bf16[1024,512]{1,0:T(8,128)(2,1)S(1)}, bf16[1024,512]{1,0:T(8,128)(2,1)S(1)}, u32[]{:S(2)}, u32[]{:S(2)}) collective-permute-start(bf16[1024,512]{1,0:T(8,128)(2,1)S(1)} %get-tuple-element.30), channel_id=1, source_target_pairs={{0,1},{1,2},{2,3},{3,4},{4,5},{5,6},{6,7},{7,8},{8,9},{9,10},{10,1... | collective-permute-start | bytes 3145736 | tf_op jit(solution)/shard_map/ppermute | solution.py:30
  48.4 1.8 fusion.39
  50.3 1.8 fusion.38
  52.2 1.8 fusion.36
  54.0 1.9 fusion.37
  55.8 1.8 fusion.50
  57.6 0.5 fusion.85
  58.1 0.8 add_add_fusion
  58.9 1.5 convert_bitcast_fusion
  60.5 1.8 fusion.34
  62.3 1.1 fusion.76
  63.4 1.8 fusion.35
  65.2 27.0 %collective-permute-start.7 = (bf16[1024,512]{1,0:T(8,128)(2,1)}, bf16[1024,512]{1,0:T(8,128)(2,1)}, u32[]{:S(2)}, u32[]{:S(2)}) collective-permute-start(bf16[1024,512]{1,0:T(8,128)(2,1)} %get-tuple-element.24), channel_id=1, source_target_pairs={{0,1},{1,2},{2,3},{3,4},{4,5},{5,6},{6,7},{7,8},{8,9},{9,10},{10,1... | collective-permute-start | bytes 3145736 | tf_op jit(solution)/shard_map/ppermute | solution.py:30
  92.2 1.8 fusion.48
  94.0 1.3 fusion.8
  96.6 0.6 compare_select_fusion
  97.3 0.7 iota.11.own_ref
  97.9 16.0 %shard_map.46 = f32[8,128]{1,0:T(8,128)} custom-call(f32[8,128]{1,0:T(8,128)} %iota.11.own_ref), custom_call_target="tpu_custom_call" | custom-call | tf_op jit(solution)/shard_map/pallas_call | solution.py:170
  114.0 1.9 fusion.86
  115.9 1.9 fusion.32
  117.8 1.8 fusion.33
  119.6 1.3 fusion.81
  122.4 2.2 fusion.26
  124.6 1.9 fusion.87
  126.6 2.1 fusion.20
  129.4 3.2 %fusion.27 = (bf16[1024,512]{1,0:T(8,128)(2,1)S(1)}, bf16[1024,512]{1,0:T(8,128)(2,1)S(1)}) fusion(f32[2,2,256,512]{3,2,1,0:T(8,128)S(1)} %add_add_fusion.1, bf16[1024,512]{1,0:T(8,128)(2,1)S(1)} %copy-done.19, f32[2,2,256,512]{3,2,1,0:T(8,128)S(1)} %fusion.26, f32[]{:T(128)} %bitcast.31, f32[]{:T(128)} %bitcast.30, bf16[1024,1024]{1,0:T(8,128)(2,1)S(1)} %copy-done.5, ...), kind=kLoop, calls=%fused_computation.44 | loop fusion | flops 14680064 | bytes 14680072 | tf_op jit(solution)/shard_map/convert_element_type | solution.py:379
  132.9 2.4 fusion.68.gram_ref
  135.4 50.3 %shard_map.47.gram_ref = f32[576,8,128]{2,1,0:T(8,128)S(1)} custom-call(f32[1024,1024]{1,0:T(8,128)S(1)} %fusion.68.gram_ref), custom_call_target="tpu_custom_call" | custom-call | tf_op jit(solution)/shard_map/pallas_call | solution.py:261
  185.7 60.4 %shard_map.48 = bf16[1024,1024]{1,0:T(8,128)(2,1)} custom-call(f32[576,8,128]{2,1,0:T(8,128)S(1)} %shard_map.47.gram_ref, bf16[1024,1024]{1,0:T(8,128)(2,1)S(1)} %pad_maximum_fusion.filtered_ref), custom_call_target="tpu_custom_call" | custom-call | tf_op jit(solution)/shard_map/pallas_call | solution.py:321
  (70 shorter events, 3.3 us)
Async XLA Ops:
  0.0 7.4 %copy-start = (bf16[3,4,256,256]{3,2,1,0:T(8,128)(2,1)S(1)}, bf16[3,4,256,256]{3,2,1,0:T(8,128)(2,1)}, u32[]{:S(2)}) copy-start(bf16[3,4,256,256]{3,2,1,0:T(8,128)(2,1)} %param.6) | copy-start | bytes 4718596
  0.0 7.4 %copy-start.22 = (s32[3,4,256]{2,1,0:T(4,128)S(1)}, s32[3,4,256]{2,1,0:T(4,128)}, u32[]{:S(2)}) copy-start(s32[3,4,256]{2,1,0:T(4,128)} %param.7) | copy-start | bytes 36868
  1.8 18.1 %collective-permute-start = (bf16[1024,512]{1,0:T(8,128)(2,1)S(1)}, bf16[1024,512]{1,0:T(8,128)(2,1)S(1)}, u32[]{:S(2)}, u32[]{:S(2)}) collective-permute-start(bf16[1024,512]{1,0:T(8,128)(2,1)S(1)} %get-tuple-element.33), channel_id=1, source_target_pairs={{0,1},{1,2},{2,3},{3,4},{4,5},{5,6},{6,7},{7,8},{8,9},{9,10},{10,1... | collective-permute-start | bytes 3145736 | tf_op jit(solution)/shard_map/ppermute | solution.py:30
  2.3 17.6 %collective-permute-start.1 = (bf16[1024,512]{1,0:T(8,128)(2,1)S(1)}, bf16[1024,512]{1,0:T(8,128)(2,1)S(1)}, u32[]{:S(2)}, u32[]{:S(2)}) collective-permute-start(bf16[1024,512]{1,0:T(8,128)(2,1)S(1)} %get-tuple-element.33), channel_id=1, source_target_pairs={{1,0},{2,1},{3,2},{4,3},{5,4},{6,5},{7,6},{8,7},{9,8},{10,9},{11,1... | collective-permute-start | bytes 3145736 | tf_op jit(solution)/shard_map/ppermute | solution.py:31
  8.2 33.9 %collective-permute-start.2 = (bf16[2,2,256,256]{2,3,1,0:T(8,128)(2,1)S(1)}, bf16[2,2,256,256]{2,3,1,0:T(8,128)(2,1)S(1)}, u32[]{:S(2)}, u32[]{:S(2)}) collective-permute-start(bf16[2,2,256,256]{2,3,1,0:T(8,128)(2,1)S(1)} %bitcast.169), channel_id=1, source_target_pairs={{1,0},{2,1},{3,2},{4,3},{5,4},{6,5},{7,6},{8,7},{9,8},{10,9},{11,1... | collective-permute-start | bytes 1572872 | tf_op jit(solution)/shard_map/ppermute | solution.py:23
  11.2 41.0 %copy-start.17 = (bf16[1,2,1,256,256]{3,4,2,1,0:T(8,128)(2,1)}, bf16[1,2,1,256,256]{3,4,2,1,0:T(8,128)(2,1)S(1)}, u32[]{:S(2)}) copy-start(bf16[1,2,1,256,256]{3,4,2,1,0:T(8,128)(2,1)S(1)} %get-tuple-element.57) | copy-start | bytes 786436
  12.6 1.0 copy-start.6
  14.1 1.6 copy-start.4
  19.9 37.7 %collective-permute-start.3 = (bf16[1024,512]{1,0:T(8,128)(2,1)S(1)}, bf16[1024,512]{1,0:T(8,128)(2,1)S(1)}, u32[]{:S(2)}, u32[]{:S(2)}) collective-permute-start(bf16[1024,512]{1,0:T(8,128)(2,1)S(1)} %get-tuple-element.17), channel_id=1, source_target_pairs={{0,1},{1,2},{2,3},{3,4},{4,5},{5,6},{6,7},{7,8},{8,9},{9,10},{10,1... | collective-permute-start | bytes 3145736 | tf_op jit(solution)/shard_map/ppermute | solution.py:30
  41.6 16.5 %collective-permute-start.4 = (bf16[1024,512]{1,0:T(8,128)(2,1)S(1)}, bf16[1024,512]{1,0:T(8,128)(2,1)S(1)}, u32[]{:S(2)}, u32[]{:S(2)}) collective-permute-start(bf16[1024,512]{1,0:T(8,128)(2,1)S(1)} %get-tuple-element.17), channel_id=1, source_target_pairs={{1,0},{2,1},{3,2},{4,3},{5,4},{6,5},{7,6},{8,7},{9,8},{10,9},{11,1... | collective-permute-start | bytes 3145736 | tf_op jit(solution)/shard_map/ppermute | solution.py:31
  42.1 16.0 %copy-start.7 = (bf16[2,2,256,256]{2,3,1,0:T(8,128)(2,1)}, bf16[2,2,256,256]{2,3,1,0:T(8,128)(2,1)S(1)}, u32[]{:S(2)}) copy-start(bf16[2,2,256,256]{2,3,1,0:T(8,128)(2,1)S(1)} %collective-permute-done.2) | copy-start | bytes 1572868
  43.2 7.1 %copy-start.18 = (bf16[1024,512]{1,0:T(8,128)(2,1)}, bf16[1024,512]{1,0:T(8,128)(2,1)S(1)}, u32[]{:S(2)}) copy-start(bf16[1024,512]{1,0:T(8,128)(2,1)S(1)} %get-tuple-element.30) | copy-start | bytes 3145732
  43.2 22.0 %collective-permute-start.5 = (bf16[1024,512]{1,0:T(8,128)(2,1)S(1)}, bf16[1024,512]{1,0:T(8,128)(2,1)S(1)}, u32[]{:S(2)}, u32[]{:S(2)}) collective-permute-start(bf16[1024,512]{1,0:T(8,128)(2,1)S(1)} %get-tuple-element.30), channel_id=1, source_target_pairs={{0,1},{1,2},{2,3},{3,4},{4,5},{5,6},{6,7},{7,8},{8,9},{9,10},{10,1... | collective-permute-start | bytes 3145736 | tf_op jit(solution)/shard_map/ppermute | solution.py:30
  48.4 16.9 %collective-permute-start.6 = (bf16[1024,512]{1,0:T(8,128)(2,1)S(1)}, bf16[1024,512]{1,0:T(8,128)(2,1)S(1)}, u32[]{:S(2)}, u32[]{:S(2)}) collective-permute-start(bf16[1024,512]{1,0:T(8,128)(2,1)S(1)} %get-tuple-element.30), channel_id=1, source_target_pairs={{1,0},{2,1},{3,2},{4,3},{5,4},{6,5},{7,6},{8,7},{9,8},{10,9},{11,1... | collective-permute-start | bytes 3145736 | tf_op jit(solution)/shard_map/ppermute | solution.py:31
  58.9 35.0 %copy-start.2 = (f32[2,2,256,512]{3,2,1,0:T(8,128)}, f32[2,2,256,512]{3,2,1,0:T(8,128)S(1)}, u32[]{:S(2)}) copy-start(f32[2,2,256,512]{3,2,1,0:T(8,128)S(1)} %add_add_fusion) | copy-start | bytes 6291460
  65.2 28.8 %copy-start.21 = (bf16[1024,512]{1,0:T(8,128)(2,1)}, bf16[1024,512]{1,0:T(8,128)(2,1)S(1)}, u32[]{:S(2)}) copy-start(bf16[1024,512]{1,0:T(8,128)(2,1)S(1)} %collective-permute-done.5) | copy-start | bytes 3145732
  65.2 30.1 %copy-start.20 = (bf16[1024,512]{1,0:T(8,128)(2,1)}, bf16[1024,512]{1,0:T(8,128)(2,1)S(1)}, u32[]{:S(2)}) copy-start(bf16[1024,512]{1,0:T(8,128)(2,1)S(1)} %collective-permute-done.6) | copy-start | bytes 3145732
  65.2 59.4 %collective-permute-start.7 = (bf16[1024,512]{1,0:T(8,128)(2,1)}, bf16[1024,512]{1,0:T(8,128)(2,1)}, u32[]{:S(2)}, u32[]{:S(2)}) collective-permute-start(bf16[1024,512]{1,0:T(8,128)(2,1)} %get-tuple-element.24), channel_id=1, source_target_pairs={{0,1},{1,2},{2,3},{3,4},{4,5},{5,6},{6,7},{7,8},{8,9},{9,10},{10,1... | collective-permute-start | bytes 3145736 | tf_op jit(solution)/shard_map/ppermute | solution.py:30
  92.2 34.3 %collective-permute-start.8 = (bf16[1024,512]{1,0:T(8,128)(2,1)}, bf16[1024,512]{1,0:T(8,128)(2,1)}, u32[]{:S(2)}, u32[]{:S(2)}) collective-permute-start(bf16[1024,512]{1,0:T(8,128)(2,1)} %get-tuple-element.24), channel_id=1, source_target_pairs={{1,0},{2,1},{3,2},{4,3},{5,4},{6,5},{7,6},{8,7},{9,8},{10,9},{11,1... | collective-permute-start | bytes 3145736 | tf_op jit(solution)/shard_map/ppermute | solution.py:31
  114.0 8.4 %copy-start.12 = (f32[2,2,256,512]{3,2,1,0:T(8,128)S(1)}, f32[2,2,256,512]{3,2,1,0:T(8,128)}, u32[]{:S(2)}) copy-start(f32[2,2,256,512]{3,2,1,0:T(8,128)} %fusion.37) | copy-start | bytes 6291460
  114.0 8.4 %copy-start.15 = (f32[2,2,512,256]{2,3,1,0:T(8,128)S(1)}, f32[2,2,512,256]{2,3,1,0:T(8,128)}, u32[]{:S(2)}) copy-start(f32[2,2,512,256]{2,3,1,0:T(8,128)} %fusion.50) | copy-start | bytes 6291460
  115.9 6.5 %copy-start.10 = (f32[2,2,256,512]{3,2,1,0:T(8,128)S(1)}, f32[2,2,256,512]{3,2,1,0:T(8,128)}, u32[]{:S(2)}) copy-start(f32[2,2,256,512]{3,2,1,0:T(8,128)} %fusion.38) | copy-start | bytes 6291460
  115.9 6.5 %copy-start.11 = (f32[2,2,256,512]{3,2,1,0:T(8,128)S(1)}, f32[2,2,256,512]{3,2,1,0:T(8,128)}, u32[]{:S(2)}) copy-start(f32[2,2,256,512]{3,2,1,0:T(8,128)} %fusion.36) | copy-start | bytes 6291460
  117.8 4.6 %copy-start.8 = (bf16[2,2,256,256]{2,3,1,0:T(8,128)(2,1)S(1)}, bf16[2,2,256,256]{2,3,1,0:T(8,128)(2,1)}, u32[]{:S(2)}) copy-start(bf16[2,2,256,256]{2,3,1,0:T(8,128)(2,1)} %copy-done.7) | copy-start | bytes 1572868
  117.8 4.6 %copy-start.9 = (f32[2,2,256,512]{3,2,1,0:T(8,128)S(1)}, f32[2,2,256,512]{3,2,1,0:T(8,128)}, u32[]{:S(2)}) copy-start(f32[2,2,256,512]{3,2,1,0:T(8,128)} %fusion.39) | copy-start | bytes 6291460
  122.4 4.1 %copy-start.14 = (f32[2,2,256,512]{3,2,1,0:T(8,128)S(1)}, f32[2,2,256,512]{3,2,1,0:T(8,128)}, u32[]{:S(2)}) copy-start(f32[2,2,256,512]{3,2,1,0:T(8,128)} %fusion.35) | copy-start | bytes 6291460
  122.4 4.1 %copy-start.16 = (f32[2,2,512,256]{2,3,1,0:T(8,128)S(1)}, f32[2,2,512,256]{2,3,1,0:T(8,128)}, u32[]{:S(2)}) copy-start(f32[2,2,512,256]{2,3,1,0:T(8,128)} %fusion.48) | copy-start | bytes 6291460
  124.6 2.0 copy-start.13
  126.6 2.2 copy-start.3
  126.6 2.5 %copy-start.5 = (bf16[1024,1024]{1,0:T(8,128)(2,1)S(1)}, bf16[1024,1024]{1,0:T(8,128)(2,1)}, u32[]{:S(2)}) copy-start(bf16[1024,1024]{1,0:T(8,128)(2,1)} %param.4) | copy-start | bytes 6291460
  126.6 2.8 %copy-start.19 = (bf16[1024,512]{1,0:T(8,128)(2,1)S(1)}, bf16[1024,512]{1,0:T(8,128)(2,1)}, u32[]{:S(2)}) copy-start(bf16[1024,512]{1,0:T(8,128)(2,1)} %copy-done.18) | copy-start | bytes 3145732
  135.4 110.7 %copy-start.1 = (bf16[3,4,256,256]{3,2,1,0:T(8,128)(2,1)S(1)}, bf16[3,4,256,256]{3,2,1,0:T(8,128)(2,1)}, u32[]{:S(2)}) copy-start(bf16[3,4,256,256]{3,2,1,0:T(8,128)(2,1)} %param.6) | copy-start | bytes 4718596
